TPU v7x, 512 devices: a whole 4x8x8 slice. The times are simulated.
512 devices in a mesh: row: 64 (over z, y_hi, core), col: 8 (over x, y_lo).
Axes of the slice: x: 4, y: 8 (y_hi: 4, y_lo: 2; y = y_hi * 2 + y_lo), z: 8, core: 2. Of those that a mesh axis runs over, the one named last changes fastest.
Arguments:
- bands: bfloat16 [64, 36, 1296], P('row'), may hold values from -6 to 6
- projections: bfloat16 [64, 256], P('row'), may hold values from -6 to 6
- qfunc: float32 [2, 2, 64, 1024], replicated, may hold values from -6 to 6
- species: int32 [32], replicated, may hold values from 0 to 1
- positions: float32 [3, 32], replicated, may hold values from 0 to 1
- glist: int32 [1024], replicated, may hold values from 1296 to 14255, as said below
Outputs:
- exchange: float32 [64, 36, 1296], P('row', None, 'col')
- proj_exchange: float32 [64, 256], P('row', 'col')
Inputs may be any that keep to these rules, and one draw needn't show every extreme that they name: `glist`: distinct; each index (kx 36 + ky) * 36 + kz has 1 <= kx <= 17 and kx^2 + my^2 + mz^2 <= 110, with my, mz the signed frequencies of ky, kz.
All inputs are finite; a program needn't handle non-finite values.
Results may differ from a plain program's by a relative error of at most 0.0005.
Values may be sent and summed in bfloat16 or wider, within the bound.
A program may use at most 64 MiB of HBM per device.

v0:
```python
import functools
import math

import jax
import jax.numpy as jnp
import ml_dtypes
import numpy as np
from jax import lax
from jax.experimental import pallas as pl
from jax.experimental.pallas import tpu as pltpu
from jax.sharding import PartitionSpec as P

N = 36
NG6 = 6
LG = 256
LANES = NG6 * LG
XB = 48
XO = 40
KR = 24
KA = 16
ATOMS, NH, NSPEC, NLIST = 32, 8, 2, 1024
LM = NSPEC * NH * NH
AUG = N**1.5 / (NH * math.sqrt(ATOMS))
SLOTS = 5
F32, BF16 = jnp.float32, jnp.bfloat16


def split_np(a):
    hi = a.astype(np.float32).astype(ml_dtypes.bfloat16)
    lo = (a - hi.astype(np.float64)).astype(np.float32).astype(ml_dtypes.bfloat16)
    return hi, lo


def make_tables():
    k = np.arange(19)[:, None]
    x = np.arange(N)[None, :]
    ang = 2 * np.pi * (k * x % N) / N
    fwd = np.zeros((2 * KR, XB))
    fwd[:19, :N] = np.cos(ang)
    fwd[KR : KR + 19, :N] = -np.sin(ang)
    weight = np.where((k == 0) | (k == N // 2), 1.0, 2.0) / N**3
    inv = np.zeros((XO, 2 * KR))
    inv[:N, :19] = (weight * np.cos(ang)).T
    inv[:N, KR : KR + 19] = (-weight * np.sin(ang)).T
    fh, fl = split_np(fwd)
    ih, il = split_np(inv)
    fwd3 = np.concatenate([fh, fh, fl], axis=1)
    inv3 = np.concatenate([ih, ih, il], axis=1)
    r = np.arange(6)
    z = np.arange(N)
    r_of = np.repeat(r, N)
    z_of = np.tile(z, 6)
    ang = 2 * np.pi * ((6 * r_of[:, None] * r_of[None, :] + z_of[:, None] * z_of[None, :]) % N) / N
    c = np.zeros((LG, LG))
    s = np.zeros((LG, LG))
    c[:216, :216] = np.cos(ang)
    s[:216, :216] = np.sin(ang)
    wf = np.block([[c, -s], [s, c]])
    wi = np.block([[c, s], [-s, c]])
    wfh, wfl = split_np(wf)
    wih, wil = split_np(wi)
    tw = np.zeros((16, LG), np.float32)
    for q in range(6):
        a = 2 * np.pi * (r_of * q % N) / N
        tw[q, :216] = np.cos(a)
        tw[8 + q, :216] = -np.sin(a)
    kern = np.zeros((NG6 * KR, LG), np.float32)
    sg = lambda v: np.where(v > N // 2, v - N, v)
    for q in range(6):
        ky = q + 6 * r_of
        for kx in range(19):
            n2 = kx**2 + sg(ky) ** 2 + sg(z_of) ** 2
            kern[q * KR + kx, :216] = np.where(n2 > 0, N**1.5 / 4 / np.maximum(n2, 1), 0)
    kk = np.arange(256)[:, None]
    col = np.arange(LM)[None, :]
    rl = (kk % NH == (col % 64) // NH).astype(np.float32)
    rm = (kk % NH == col % NH).astype(np.float32)
    rep = np.concatenate([rl, rm], axis=1).astype(ml_dtypes.bfloat16)
    rsum = rl.T.astype(ml_dtypes.bfloat16)
    return dict(fwd3=fwd3, inv3=inv3, wfh=wfh, wfl=wfl, wih=wih, wil=wil, tw=tw, kern=kern, rep=rep, rsum=rsum)


TABLES = make_tables()
TABLE_NAMES = ("fwd3", "inv3", "wfh", "wfl", "wih", "wil", "tw", "kern", "rep", "rsum")


def split(a):
    hi = a.astype(BF16)
    return hi, (a - hi.astype(F32)).astype(BF16)


def mm(a, b):
    return jnp.dot(a, b, preferred_element_type=F32)


def mm_nt(a, b):
    return lax.dot_general(a, b, (((1,), (1,)), ((), ())), preferred_element_type=F32)


def dft3(a, b, c, sign):
    h = math.sqrt(3.0) / 2
    sr, si = b[0] + c[0], b[1] + c[1]
    dr, di = (b[0] - c[0]) * h, (b[1] - c[1]) * h
    tr, ti = a[0] - 0.5 * sr, a[1] - 0.5 * si
    zero = (a[0] + sr, a[1] + si)
    minus = (tr + di, ti - dr)
    plus = (tr - di, ti + dr)
    return (zero, minus, plus) if sign < 0 else (zero, plus, minus)


def dft6(v, sign):
    add = lambda p, q: (p[0] + q[0], p[1] + q[1])
    sub = lambda p, q: (p[0] - q[0], p[1] - q[1])
    e = dft3(add(v[0], v[3]), add(v[1], v[4]), add(v[2], v[5]), sign)
    o = dft3(sub(v[0], v[3]), sub(v[4], v[1]), sub(v[2], v[5]), sign)
    return [e[0], o[2], e[1], o[0], e[2], o[1]]


def pair_indices(special, x):
    one = jnp.where(special, 0, 1)
    first = (jnp.where(special, x, 0), one, jnp.where(special, 1 - x, 0), one, 1)
    second = (2, jnp.where(special, 0, 2), 3, jnp.where(special, 1, 3), 1)
    return first, second


def setup_lists(glist_ref, positions_ref, species_ref, yzt_ref, phase_ref, choose_ref):
    g = glist_ref[...]
    kx = g // (N * N)
    ky = g // N % N
    kz = g % N
    where = (ky % 6) * LG + (ky // 6) * N + kz
    step = 256
    for base in range(0, LANES, step):
        rows = lax.broadcasted_iota(jnp.int32, (step, NLIST), 0) + base
        yzt_ref[base : base + step, :] = jnp.where(rows == where, 1.0, 0.0).astype(BF16)
    sg = lambda v: jnp.where(v > N // 2, v - N, v).astype(F32)
    eye = lax.broadcasted_iota(jnp.int32, (ATOMS, ATOMS), 0) == lax.broadcasted_iota(jnp.int32, (ATOMS, ATOMS), 1)
    column = lambda row: jnp.sum(jnp.where(eye, row, 0.0), axis=1, keepdims=True)
    turns = (
        column(positions_ref[0:1, :]) * kx.astype(F32)
        + column(positions_ref[1:2, :]) * sg(ky)
        + column(positions_ref[2:3, :]) * sg(kz)
    )
    theta = (turns - jnp.floor(turns)) * (2.0 * math.pi)
    phase_ref[0] = jnp.cos(theta)
    phase_ref[1] = -jnp.sin(theta)
    spec = column(species_ref[...].astype(F32))
    of_lane = lax.broadcasted_iota(jnp.int32, (ATOMS, LM), 1) // (NH * NH)
    choose_ref[...] = jnp.where(spec == of_lane.astype(F32), 1.0, 0.0)


def expand_coef(coef_ref, b, rep_ref, exp_ref):
    row = coef_ref[b].astype(F32)
    own = lax.broadcasted_iota(jnp.int32, (ATOMS, 256), 1) // NH == lax.broadcasted_iota(jnp.int32, (ATOMS, 256), 0)
    exp_ref[b] = mm(jnp.where(own, row, 0.0).astype(BF16), rep_ref[...])


def kx_of_rows(glist_ref):
    kx = glist_ref[...] // (N * N)
    rows = lax.broadcasted_iota(jnp.int32, (SLOTS * 2 * KA, NLIST), 0) % KA
    return rows == kx


def augment(first, second, glist_ref, qs_ref, exp_ref, choose_ref, phase_ref, yzt_ref, faug_ref):
    mixed = jnp.concatenate(
        [exp_ref[i][:, :LM] * exp_ref[j][:, LM:] * choose_ref[...] for i, j in zip(first, second)], axis=0
    )
    hi, lo = split(mixed)
    rows = []
    zs = []
    for c in range(2):
        qh, ql = split(qs_ref[c])
        zs.append(mm(hi, qh) + mm(lo, qh) + mm(hi, ql))
    z_re, z_im = zs
    for t in range(SLOTS):
        zr, zi = z_re[t * ATOMS : (t + 1) * ATOMS], z_im[t * ATOMS : (t + 1) * ATOMS]
        rows.append(jnp.sum(phase_ref[0] * zr - phase_ref[1] * zi, axis=0, keepdims=True) * AUG)
        rows.append(jnp.sum(phase_ref[0] * zi + phase_ref[1] * zr, axis=0, keepdims=True) * AUG)
    spread = jnp.concatenate([jnp.broadcast_to(row, (KA, NLIST)) for row in rows], axis=0)
    spread = jnp.where(kx_of_rows(glist_ref), spread, 0.0)
    hi, lo = split(spread)
    for base in range(0, LANES, LG):
        part = yzt_ref[base : base + LG, :]
        faug_ref[:, base : base + LG] = mm_nt(hi, part) + mm_nt(lo, part)


def pairs(slots, first, second, band_ref, faug_ref, wst_ref, acc_ref, lhs_ref, tabs):
    n = len(slots)
    for m, t in enumerate(slots):
        rho = band_ref[first[t]].astype(F32) * band_ref[second[t]].astype(F32)
        hi, lo = split(rho)
        spec = mm(tabs["fwd3"][...], jnp.concatenate([hi, lo, hi], axis=0))
        v = [
            (spec[:KR, g * LG : (g + 1) * LG], spec[KR:, g * LG : (g + 1) * LG]) for g in range(NG6)
        ]
        for q, (re, im) in enumerate(dft6(v, -1)):
            if q:
                cr, ci = tabs["tw"][q : q + 1, :], tabs["tw"][8 + q : 9 + q, :]
                re, im = re * cr - im * ci, re * ci + im * cr
            at = (q * n + m) * KR
            lhs_ref[at : at + KR, :LG] = re
            lhs_ref[at : at + KR, LG:] = im
    rows = NG6 * n * KR
    hi, lo = split(lhs_ref[:rows, :])
    f = mm(hi, tabs["wfh"][...]) + mm(lo, tabs["wfh"][...]) + mm(hi, tabs["wfl"][...])
    for q in range(NG6):
        kern = tabs["kern"][q * KR : (q + 1) * KR, :]
        for m, t in enumerate(slots):
            at = (q * n + m) * KR
            for c in range(2):
                w = f[at : at + KR, c * LG : (c + 1) * LG]
                a = (t * 2 + c) * KA
                low = (w[:KA] + faug_ref[a : a + KA, q * LG : (q + 1) * LG]) * kern[:KA]
                wst_ref[a : a + KA, q * LG : (q + 1) * LG] = low
                lhs_ref[at : at + KA, c * LG : (c + 1) * LG] = low
                lhs_ref[at + KA : at + KR, c * LG : (c + 1) * LG] = w[KA:] * kern[KA:]
    hi, lo = split(lhs_ref[:rows, :])
    f = mm(hi, tabs["wih"][...]) + mm(lo, tabs["wih"][...]) + mm(hi, tabs["wil"][...])
    for m, t in enumerate(slots):
        v = []
        for q in range(NG6):
            at = (q * n + m) * KR
            re, im = f[at : at + KR, :LG], f[at : at + KR, LG:]
            if q:
                cr, ci = tabs["tw"][q : q + 1, :], tabs["tw"][8 + q : 9 + q, :]
                re, im = re * cr + im * ci, im * cr - re * ci
            v.append((re, im))
        v = dft6(v, 1)
        w = jnp.concatenate([jnp.concatenate([p[0], p[1]], axis=0) for p in v], axis=1)
        hi, lo = split(w)
        pot = mm(tabs["inv3"][...], jnp.concatenate([hi, lo, hi], axis=0))
        i, j = first[t], second[t]
        acc_ref[i] += pot * band_ref[j].astype(F32)[:XO]
        twice = jnp.where(jnp.int32(i) == jnp.int32(j), 0.0, 1.0)
        acc_ref[j] += pot * band_ref[i].astype(F32)[:XO] * twice


def slopes(slots, first, second, glist_ref, qs_ref, exp_ref, choose_ref, phase_ref, yzt_ref, wst_ref, pacc_ref):
    hi, lo = split(wst_ref[...])
    picked = mm(hi, yzt_ref[...]) + mm(lo, yzt_ref[...])
    picked = jnp.where(kx_of_rows(glist_ref), picked, 0.0)
    re_rows, im_rows = [], []
    for t in range(SLOTS):
        a = t * 2 * KA
        wr = jnp.sum(picked[a : a + KA], axis=0, keepdims=True)
        wi = jnp.sum(picked[a + KA : a + 2 * KA], axis=0, keepdims=True)
        re_rows.append(wr * phase_ref[0] + wi * phase_ref[1])
        im_rows.append(wi * phase_ref[0] - wr * phase_ref[1])
    total = None
    for c, cross in enumerate((re_rows, im_rows)):
        ch, cl = split(jnp.concatenate(cross, axis=0))
        qh, ql = split(qs_ref[c])
        part = mm_nt(ch, qh) + mm_nt(cl, qh) + mm_nt(ch, ql)
        total = part if total is None else total + part
    total = total * (2.0 * AUG / N**3)
    for t in range(SLOTS):
        slope = total[t * ATOMS : (t + 1) * ATOMS] * choose_ref[...]
        i, j = first[t], second[t]

        def give(slope=slope, i=i, j=j):
            pacc_ref[i] += slope * exp_ref[j][:, LM:]
            twice = jnp.where(jnp.int32(i) == jnp.int32(j), 0.0, 1.0)
            pacc_ref[j] += slope * exp_ref[i][:, LM:] * twice

        if t in slots:
            give()
        else:
            pl.when(slots[t])(give)


def coef_rows(pacc_ref, rsum_ref):
    own = lax.broadcasted_iota(jnp.int32, (ATOMS, 256), 1) // NH == lax.broadcasted_iota(jnp.int32, (ATOMS, 256), 0)
    out = []
    for b in range(4):
        hi, lo = split(pacc_ref[b])
        full = mm(hi, rsum_ref[...]) + mm(lo, rsum_ref[...])
        out.append(jnp.sum(jnp.where(own, full, 0.0), axis=0, keepdims=True))
    return out


def local_kernel(*refs):
    nt = len(TABLE_NAMES)
    (meta_ref, band_ref, coef_ref, qs_ref, species_ref, positions_ref, glist_ref) = refs[:7]
    tabs = dict(zip(TABLE_NAMES, refs[7 : 7 + nt]))
    acc_ref = refs[7 + nt]
    (yzt_ref, phase_ref, choose_ref, exp_ref, faug_ref, wst_ref, lhs_ref, pacc_ref) = refs[8 + nt :]
    special = meta_ref[0] == 1
    x = meta_ref[1]
    setup_lists(glist_ref, positions_ref, species_ref, yzt_ref, phase_ref, choose_ref)
    for b in range(4):
        expand_coef(coef_ref, b, tabs["rep"], exp_ref)
    first, second = pair_indices(special, x)
    acc_ref[...] = jnp.zeros_like(acc_ref)
    pacc_ref[...] = jnp.zeros_like(pacc_ref)
    wst_ref[...] = jnp.zeros_like(wst_ref)
    augment(first, second, glist_ref, qs_ref, exp_ref, choose_ref, phase_ref, yzt_ref, faug_ref)
    run = functools.partial(pairs, first=first, second=second, band_ref=band_ref, faug_ref=faug_ref,
                            wst_ref=wst_ref, acc_ref=acc_ref, lhs_ref=lhs_ref, tabs=tabs)
    run((0, 1))
    run((2, 3))
    pl.when(special)(lambda: run((4,)))
    slopes(SlotSet(special), first, second, glist_ref, qs_ref,
           exp_ref, choose_ref, phase_ref, yzt_ref, wst_ref, pacc_ref)
    for b, row in enumerate(coef_rows(pacc_ref, tabs["rsum"])):
        acc_ref[b, N : N + 1, :LG] = row


class SlotSet:
    def __init__(self, special):
        self.special = special

    def __contains__(self, t):
        return t < 4

    def __getitem__(self, t):
        return self.special


def local_call(meta, bands4, coefs4, qs, species, positions, glist):
    vm = pl.BlockSpec(memory_space=pltpu.VMEM)
    return pl.pallas_call(
        local_kernel,
        out_shape=jax.ShapeDtypeStruct((4, XO, LANES), F32),
        in_specs=[pl.BlockSpec(memory_space=pltpu.SMEM)] + [vm] * (6 + len(TABLE_NAMES)),
        out_specs=vm,
        scratch_shapes=[
            pltpu.VMEM((LANES, NLIST), BF16),
            pltpu.VMEM((2, ATOMS, NLIST), F32),
            pltpu.VMEM((ATOMS, LM), F32),
            pltpu.VMEM((4, ATOMS, 2 * LM), F32),
            pltpu.VMEM((SLOTS * 2 * KA, LANES), F32),
            pltpu.VMEM((SLOTS * 2 * KA, LANES), F32),
            pltpu.VMEM((2 * NG6 * KR, 2 * LG), F32),
            pltpu.VMEM((4, ATOMS, LM), F32),
        ],
        compiler_params=pltpu.CompilerParams(vmem_limit_bytes=48 * 2**20),
    )(meta, bands4, coefs4, qs, species.reshape(1, ATOMS), positions, glist.reshape(1, NLIST),
      *[jnp.asarray(TABLES[name]) for name in TABLE_NAMES])


def offset_of(slot):
    return slot + 1 if slot % 2 == 0 or slot == 15 else 32 - (slot + 1)


def on_device(bands, projections, qfunc, species, positions, glist):
    row, col = lax.axis_index("row"), lax.axis_index("col")
    group, core = row // 2, row % 2
    slot = col * 2 + core
    special = slot == 15
    x = jnp.where(group >= 16, 1, 0)
    meta = jnp.stack([special.astype(jnp.int32), x.astype(jnp.int32)])
    dev = lambda g, c, k: ((g % 32) * 2 + k) * 8 + c
    ids = [(g, c, k) for g in range(32) for c in range(8) for k in range(2)]
    sib = [(dev(g, c, k), dev(g, c, 1 - k)) for g, c, k in ids]
    near = [(dev(g, c, k), dev(g - offset_of(2 * c + k), c, k)) for g, c, k in ids]
    far = [(dev(g, c, k), dev(g - offset_of(2 * c + 1 - k), c, 1 - k)) for g, c, k in ids]
    back = [(b, a) for a, b in near]
    axes = ("row", "col")
    field = jnp.pad(bands[0].reshape(N, NG6, 216), ((0, XB - N), (0, 0), (0, LG - 216))).reshape(XB, LANES)
    coef = projections
    parts = [(field, coef)] + [(lax.ppermute(field, axes, p), lax.ppermute(coef, axes, p)) for p in (sib, near, far)]
    bands4 = jnp.stack([p[0] for p in parts])
    coefs4 = jnp.stack([p[1] for p in parts])
    q5 = qfunc.reshape(2, NSPEC, NH, NH, NLIST)
    qs = (0.5 * (q5 + jnp.swapaxes(q5, 2, 3))).reshape(2, LM, NLIST)
    acc = local_call(meta, bands4, coefs4, qs, species, positions, glist)
    got = lax.ppermute(acc[2:], axes, back)
    mine = acc[:2] + got
    total = mine[0] + lax.ppermute(mine[1], axes, sib)
    grid = total[:N].reshape(N, NG6, LG)[:, :, :216].reshape(N, 8, 162).transpose(1, 0, 2)
    proj = total[N, :LG].reshape(8, 32)
    grid = lax.all_to_all(grid, "col", 0, 0, tiled=True)
    proj = lax.all_to_all(proj, "col", 0, 0, tiled=True)
    return (-0.5 * jnp.sum(grid.reshape(8, N, 162), axis=0)[None], -0.5 * jnp.sum(proj.reshape(8, 32), axis=0)[None])


def solution(mesh):
    return jax.shard_map(
        on_device,
        mesh=mesh,
        in_specs=(P("row", None, None), P("row", None), P(), P(), P(), P()),
        out_specs=(P("row", None, "col"), P("row", "col")),
        check_vma=False,
    )
```

profile of v0, /device:TPU:16, one launch (start us, length us, event | category | flops | bytes accessed | tf_op | source)
XLA Modules:
  0.0 139.1 jit_solution(151677586975850674)
XLA Ops:
  0.6 1.9 %collective-permute-start.3 = (bf16[1,256]{1,0:T(2,128)(2,1)}, bf16[1,256]{1,0:T(2,128)(2,1)S(1)}, u32[]{:S(2)}, u32[]{:S(2)}) collective-permute-start(bf16[1,256]{1,0:T(2,128)(2,1)} %param.17), channel_id=1, source_target_pairs={{0,8},{8,0},{1,9},{9,1},{2,10},{10,2},{3,11},{11,3},{4,12},{12,4},... | collective-permute-start | bytes 1544 | tf_op jit(solution)/shard_map/ppermute | solution.py:361
  2.6 6.0 %collective-permute-start.5 = (bf16[1,256]{1,0:T(2,128)(2,1)}, bf16[1,256]{1,0:T(2,128)(2,1)S(1)}, u32[]{:S(2)}, u32[]{:S(2)}) collective-permute-start(bf16[1,256]{1,0:T(2,128)(2,1)} %param.17), channel_id=1, source_target_pairs={{0,40},{8,496},{1,73},{9,465},{2,106},{10,434},{3,139},{11,403},{4... | collective-permute-start | bytes 1544 | tf_op jit(solution)/shard_map/ppermute | solution.py:361
  8.6 4.0 %collective-permute-start.4 = (bf16[1,256]{1,0:T(2,128)(2,1)}, bf16[1,256]{1,0:T(2,128)(2,1)S(1)}, u32[]{:S(2)}, u32[]{:S(2)}) collective-permute-start(bf16[1,256]{1,0:T(2,128)(2,1)} %param.17), channel_id=1, source_target_pairs={{0,496},{8,40},{1,465},{9,73},{2,434},{10,106},{3,403},{11,139},{4... | collective-permute-start | bytes 1544 | tf_op jit(solution)/shard_map/ppermute | solution.py:361
  12.7 1.1 reshape_squeeze.4
  13.8 3.2 %collective-permute-start.2 = (bf16[48,1536]{1,0:T(8,128)(2,1)S(1)}, bf16[48,1536]{1,0:T(8,128)(2,1)S(1)}, u32[]{:S(2)}, u32[]{:S(2)}) collective-permute-start(bf16[48,1536]{1,0:T(8,128)(2,1)S(1)} %bitcast.42), channel_id=1, source_target_pairs={{0,40},{8,496},{1,73},{9,465},{2,106},{10,434},{3,139},{11,403},{4... | collective-permute-start | bytes 442376 | tf_op jit(solution)/shard_map/ppermute | solution.py:361
  17.1 7.4 %collective-permute-start.1 = (bf16[48,1536]{1,0:T(8,128)(2,1)S(1)}, bf16[48,1536]{1,0:T(8,128)(2,1)S(1)}, u32[]{:S(2)}, u32[]{:S(2)}) collective-permute-start(bf16[48,1536]{1,0:T(8,128)(2,1)S(1)} %bitcast.43), channel_id=1, source_target_pairs={{0,496},{8,40},{1,465},{9,73},{2,434},{10,106},{3,403},{11,139},{4... | collective-permute-start | bytes 442376 | tf_op jit(solution)/shard_map/ppermute | solution.py:361
  24.6 2.5 %fusion = f32[2,2,8,8,1024]{4,3,2,1,0:T(8,128)S(1)} fusion(f32[2,2,8,8,1024]{4,3,2,1,0:T(8,128)} %bitcast.37), kind=kLoop, calls=%fused_computation.1 | loop fusion | flops 524288 | bytes 2097152 | tf_op jit(solution)/shard_map/mul | solution.py:365
  27.0 2.0 %collective-permute-start = (bf16[48,1536]{1,0:T(8,128)(2,1)S(1)}, bf16[48,1536]{1,0:T(8,128)(2,1)S(1)}, u32[]{:S(2)}, u32[]{:S(2)}) collective-permute-start(bf16[48,1536]{1,0:T(8,128)(2,1)S(1)} %bitcast.44), channel_id=1, source_target_pairs={{0,8},{8,0},{1,9},{9,1},{2,10},{10,2},{3,11},{11,3},{4,12},{12,4},... | collective-permute-start | bytes 442376 | tf_op jit(solution)/shard_map/ppermute | solution.py:361
  29.1 0.1 pad_add_fusion.refs_0_
  29.2 0.2 stack_reshape.3
  29.4 0.7 copy-done.13
  30.1 0.2 collective-permute-done
  30.3 0.1 pad_maximum_fusion.refs_1_
  30.5 0.9 copy-done
  31.3 0.2 copy-done.1
  31.5 0.0 copy-done.5
  31.5 12.3 %shard_map.167 = f32[4,40,1536]{2,1,0:T(8,128)S(1)} custom-call(s32[2]{0:T(128)S(1)} %pad_add_fusion.refs_0_, bf16[4,48,1536]{2,1,0:T(8,128)(2,1)S(1)} %pad_maximum_fusion.refs_1_, bf16[4,1,256]{2,1,0:T(2,128)(2,1)S(1)} %pad_maximum_fusion.1.refs_2_, f32[2,128,1024]{2,1,0:T(8,128)S(1)} %bitcast.31, s32[1,32]{1,0:T(1,128)S(1)} %bitcast.33, ...), custom_call_target="tpu_custom_call" | custom-call | tf_op jit(solution)/shard_map/pallas_call | solution.py:321
  43.9 1.9 %collective-permute-start.6 = (f32[2,40,1536]{2,1,0:T(8,128)S(1)}, f32[2,40,1536]{2,1,0:T(8,128)S(1)}, u32[]{:S(2)}, u32[]{:S(2)}) collective-permute-start(f32[2,40,1536]{2,1,0:T(8,128)S(1)} %slice.29), channel_id=1, source_target_pairs={{496,0},{40,8},{465,1},{73,9},{434,2},{106,10},{403,3},{139,11},{3... | collective-permute-start | bytes 1474568 | tf_op jit(solution)/shard_map/ppermute | solution.py:367
  45.8 9.7 %collective-permute-done.6 = f32[2,40,1536]{2,1,0:T(8,128)S(1)} collective-permute-done((f32[2,40,1536]{2,1,0:T(8,128)S(1)}, f32[2,40,1536]{2,1,0:T(8,128)S(1)}, u32[]{:S(2)}, u32[]{:S(2)}) %collective-permute-start.6) | collective-permute-done | bytes 491552 | tf_op jit(solution)/shard_map/ppermute | solution.py:367
  55.5 0.1 slice_add_fusion
  55.6 14.6 %collective-permute-start.7 = (f32[40,1536]{1,0:T(8,128)S(1)}, f32[40,1536]{1,0:T(8,128)S(1)}, u32[]{:S(2)}, u32[]{:S(2)}) collective-permute-start(f32[40,1536]{1,0:T(8,128)S(1)} %slice_bitcast_fusion), channel_id=1, source_target_pairs={{0,8},{8,0},{1,9},{9,1},{2,10},{10,2},{3,11},{11,3},{4,12},{12,4},... | collective-permute-start | bytes 737288 | tf_op jit(solution)/shard_map/ppermute | solution.py:369
  70.2 1.1 collective-permute-done.7
  71.4 0.7 all_to_all.10
  72.0 49.3 %all-to-all-start.1 = ((f32[8,1,32]{2,1,0:T(1,128)}), f32[8,1,32]{2,1,0:T(1,128)S(1)}, u32[]{:S(2)}, u32[]{:S(2)}) async-start(f32[8,1,32]{2,1,0:T(1,128)} %bitcast.17), calls=%async_computation.1 | async-start | bytes 8192 | tf_op jit(solution)/shard_map/all_to_all | solution.py:373
  121.4 0.1 reshape.53
  121.4 0.2 reshape.54
  121.7 0.8 copy.21
  122.5 5.0 %all-to-all-done.1 = f32[8,1,32]{2,1,0:T(1,128)S(1)} async-done(((f32[8,1,32]{2,1,0:T(1,128)}), f32[8,1,32]{2,1,0:T(1,128)S(1)}, u32[]{:S(2)}, u32[]{:S(2)}) %all-to-all-start.1) | async-done | bytes 1056 | tf_op jit(solution)/shard_map/all_to_all | solution.py:373
  127.5 3.4 %all-to-all-start = ((f32[8,36,162]{2,1,0:T(8,128)}), f32[8,36,162]{2,1,0:T(8,128)S(1)}, u32[]{:S(2)}, u32[]{:S(2)}) async-start(f32[8,36,162]{2,1,0:T(8,128)} %copy.21), calls=%async_computation | async-start | bytes 655360 | tf_op jit(solution)/shard_map/all_to_all | solution.py:372
  130.9 0.5 multiply_bitcast_fusion
  131.4 7.0 %all-to-all-done = f32[8,36,162]{2,1,0:T(8,128)S(1)} async-done(((f32[8,36,162]{2,1,0:T(8,128)}), f32[8,36,162]{2,1,0:T(8,128)S(1)}, u32[]{:S(2)}, u32[]{:S(2)}) %all-to-all-start) | async-done | bytes 186656 | tf_op jit(solution)/shard_map/all_to_all | solution.py:372
  138.5 0.6 mul.48
  (39 shorter events, 0.3 us)
Async XLA Ops:
  0.6 26.4 %collective-permute-start.3 = (bf16[1,256]{1,0:T(2,128)(2,1)}, bf16[1,256]{1,0:T(2,128)(2,1)S(1)}, u32[]{:S(2)}, u32[]{:S(2)}) collective-permute-start(bf16[1,256]{1,0:T(2,128)(2,1)} %param.17), channel_id=1, source_target_pairs={{0,8},{8,0},{1,9},{9,1},{2,10},{10,2},{3,11},{11,3},{4,12},{12,4},... | collective-permute-start | bytes 1544 | tf_op jit(solution)/shard_map/ppermute | solution.py:361
  2.6 26.8 %collective-permute-start.5 = (bf16[1,256]{1,0:T(2,128)(2,1)}, bf16[1,256]{1,0:T(2,128)(2,1)S(1)}, u32[]{:S(2)}, u32[]{:S(2)}) collective-permute-start(bf16[1,256]{1,0:T(2,128)(2,1)} %param.17), channel_id=1, source_target_pairs={{0,40},{8,496},{1,73},{9,465},{2,106},{10,434},{3,139},{11,403},{4... | collective-permute-start | bytes 1544 | tf_op jit(solution)/shard_map/ppermute | solution.py:361
  8.6 20.8 %collective-permute-start.4 = (bf16[1,256]{1,0:T(2,128)(2,1)}, bf16[1,256]{1,0:T(2,128)(2,1)S(1)}, u32[]{:S(2)}, u32[]{:S(2)}) collective-permute-start(bf16[1,256]{1,0:T(2,128)(2,1)} %param.17), channel_id=1, source_target_pairs={{0,496},{8,40},{1,465},{9,73},{2,434},{10,106},{3,403},{11,139},{4... | collective-permute-start | bytes 1544 | tf_op jit(solution)/shard_map/ppermute | solution.py:361
  13.8 16.2 %collective-permute-start.2 = (bf16[48,1536]{1,0:T(8,128)(2,1)S(1)}, bf16[48,1536]{1,0:T(8,128)(2,1)S(1)}, u32[]{:S(2)}, u32[]{:S(2)}) collective-permute-start(bf16[48,1536]{1,0:T(8,128)(2,1)S(1)} %bitcast.42), channel_id=1, source_target_pairs={{0,40},{8,496},{1,73},{9,465},{2,106},{10,434},{3,139},{11,403},{4... | collective-permute-start | bytes 442376 | tf_op jit(solution)/shard_map/ppermute | solution.py:361
  17.1 13.0 %collective-permute-start.1 = (bf16[48,1536]{1,0:T(8,128)(2,1)S(1)}, bf16[48,1536]{1,0:T(8,128)(2,1)S(1)}, u32[]{:S(2)}, u32[]{:S(2)}) collective-permute-start(bf16[48,1536]{1,0:T(8,128)(2,1)S(1)} %bitcast.43), channel_id=1, source_target_pairs={{0,496},{8,40},{1,465},{9,73},{2,434},{10,106},{3,403},{11,139},{4... | collective-permute-start | bytes 442376 | tf_op jit(solution)/shard_map/ppermute | solution.py:361
  24.5 5.9 %copy-start.2 = (bf16[512,512]{1,0:T(8,128)(2,1)S(1)}, bf16[512,512]{1,0:T(8,128)(2,1)}, u32[]{:S(2)}) copy-start(bf16[512,512]{1,0:T(8,128)(2,1)} %constant.71.clone.refs_10_) | copy-start | bytes 1572868
  24.5 5.9 %copy-start.3 = (bf16[512,512]{1,0:T(8,128)(2,1)S(1)}, bf16[512,512]{1,0:T(8,128)(2,1)}, u32[]{:S(2)}) copy-start(bf16[512,512]{1,0:T(8,128)(2,1)} %constant.70.clone.refs_9_) | copy-start | bytes 1572868
  27.0 3.3 %collective-permute-start = (bf16[48,1536]{1,0:T(8,128)(2,1)S(1)}, bf16[48,1536]{1,0:T(8,128)(2,1)S(1)}, u32[]{:S(2)}, u32[]{:S(2)}) collective-permute-start(bf16[48,1536]{1,0:T(8,128)(2,1)S(1)} %bitcast.44), channel_id=1, source_target_pairs={{0,8},{8,0},{1,9},{9,1},{2,10},{10,2},{3,11},{11,3},{4,12},{12,4},... | collective-permute-start | bytes 442376 | tf_op jit(solution)/shard_map/ppermute | solution.py:361
  29.1 1.3 copy-start.4
  29.1 1.3 copy-start.6
  29.2 1.3 copy-start.7
  29.2 1.3 copy-start.8
  29.2 1.3 copy-start.9
  29.2 1.3 copy-start.11
  29.4 0.7 copy-start.13
  30.3 1.0 copy-start
  30.3 1.2 copy-start.1
  30.3 1.2 copy-start.5
  30.4 1.1 copy-start.10
  30.4 1.1 copy-start.12
  43.9 11.6 %collective-permute-start.6 = (f32[2,40,1536]{2,1,0:T(8,128)S(1)}, f32[2,40,1536]{2,1,0:T(8,128)S(1)}, u32[]{:S(2)}, u32[]{:S(2)}) collective-permute-start(f32[2,40,1536]{2,1,0:T(8,128)S(1)} %slice.29), channel_id=1, source_target_pairs={{496,0},{40,8},{465,1},{73,9},{434,2},{106,10},{403,3},{139,11},{3... | collective-permute-start | bytes 1474568 | tf_op jit(solution)/shard_map/ppermute | solution.py:367
  55.6 15.7 %collective-permute-start.7 = (f32[40,1536]{1,0:T(8,128)S(1)}, f32[40,1536]{1,0:T(8,128)S(1)}, u32[]{:S(2)}, u32[]{:S(2)}) collective-permute-start(f32[40,1536]{1,0:T(8,128)S(1)} %slice_bitcast_fusion), channel_id=1, source_target_pairs={{0,8},{8,0},{1,9},{9,1},{2,10},{10,2},{3,11},{11,3},{4,12},{12,4},... | collective-permute-start | bytes 737288 | tf_op jit(solution)/shard_map/ppermute | solution.py:369
  72.0 55.4 %all-to-all-start.1 = ((f32[8,1,32]{2,1,0:T(1,128)}), f32[8,1,32]{2,1,0:T(1,128)S(1)}, u32[]{:S(2)}, u32[]{:S(2)}) async-start(f32[8,1,32]{2,1,0:T(1,128)} %bitcast.17), calls=%async_computation.1 | async-start | bytes 8192 | tf_op jit(solution)/shard_map/all_to_all | solution.py:373
  127.5 11.0 %all-to-all-start = ((f32[8,36,162]{2,1,0:T(8,128)}), f32[8,36,162]{2,1,0:T(8,128)S(1)}, u32[]{:S(2)}, u32[]{:S(2)}) async-start(f32[8,36,162]{2,1,0:T(8,128)} %copy.21), calls=%async_computation | async-start | bytes 655360 | tf_op jit(solution)/shard_map/all_to_all | solution.py:372
where the time goes:
time: 140 us; the launch traced here: 139 us
  starting transfers between devices  93.9 us (67%)
  waiting for transfers between devices  23 us (16%)
  Pallas kernels  12.3 us (9%)
  local copies, waits for them, and re-layouts  5.57 us (4%)
  other arithmetic  3.28 us (2%)
    all_to_all x1, starting transfers between devices, on_device(): proj = lax.all_to_all(proj, 'col', 0, 0, tiled=True)  49.3 us
    ppermute x1, starting transfers between devices, on_device(): total = mine[0] + lax.ppermute(mine[1], axes, sib)  14.6 us
    ppermute x3, starting transfers between devices, on_device(): lax.ppermute(field, axes, p)  12.7 us
    pallas_call x1, Pallas kernels, local_call(): pl.pallas_call(local_kernel, out_shape=jax.ShapeDtypeStruct((4, XO, LANES...  12.3 us
    ppermute x3, starting transfers between devices, on_device(): lax.ppermute(coef, axes, p)  12 us
    ppermute x1, waiting for transfers between devices, on_device(): got = lax.ppermute(acc[2:], axes, back)  9.69 us
    all_to_all x1, waiting for transfers between devices, on_device(): grid = lax.all_to_all(grid, 'col', 0, 0, tiled=True)  7.03 us
    all_to_all x1, waiting for transfers between devices, on_device(): proj = lax.all_to_all(proj, 'col', 0, 0, tiled=True)  4.99 us
  transfers between devices with their start and end apart: 10, of which 5 were waited for; matrix products, arithmetic and copies ran while one was open for 4% of the time, Pallas kernels for 0%

commit v1 on v0

--- a/solution.py
+++ b/solution.py
@@ -22,6 +22,8 @@
 LM = NSPEC * NH * NH
 AUG = N**1.5 / (NH * math.sqrt(ATOMS))
 SLOTS = 5
+TAIL = 384
+CHUNK = 162
 F32, BF16 = jnp.float32, jnp.bfloat16
 
 
@@ -76,12 +78,13 @@
     rl = (kk % NH == (col % 64) // NH).astype(np.float32)
     rm = (kk % NH == col % NH).astype(np.float32)
     rep = np.concatenate([rl, rm], axis=1).astype(ml_dtypes.bfloat16)
-    rsum = rl.T.astype(ml_dtypes.bfloat16)
-    return dict(fwd3=fwd3, inv3=inv3, wfh=wfh, wfl=wfl, wih=wih, wil=wil, tw=tw, kern=kern, rep=rep, rsum=rsum)
+    rsum = np.ascontiguousarray(rep.T)
+    dft = np.stack([wfh, wfl, wih, wil])
+    return dict(fwd3=fwd3, inv3=inv3, dft=dft, tw=tw, kern=kern, rep=rep, rsum=rsum)
 
 
 TABLES = make_tables()
-TABLE_NAMES = ("fwd3", "inv3", "wfh", "wfl", "wih", "wil", "tw", "kern", "rep", "rsum")
+TABLE_NAMES = ("fwd3", "inv3", "dft", "tw", "kern", "rep", "rsum")
 
 
 def split(a):
@@ -117,9 +120,8 @@
 
 
 def pair_indices(special, x):
-    one = jnp.where(special, 0, 1)
-    first = (jnp.where(special, x, 0), one, jnp.where(special, 1 - x, 0), one, 1)
-    second = (2, jnp.where(special, 0, 2), 3, jnp.where(special, 1, 3), 1)
+    first = (jnp.where(special, x, 0), 1, jnp.where(special, 1 - x, 0), jnp.where(special, 0, 1), 0)
+    second = (2, jnp.where(special, 1, 2), 3, jnp.where(special, 1, 3), 0)
     return first, second
 
 
@@ -149,10 +151,13 @@
     choose_ref[...] = jnp.where(spec == of_lane.astype(F32), 1.0, 0.0)
 
 
-def expand_coef(coef_ref, b, rep_ref, exp_ref):
-    row = coef_ref[b].astype(F32)
-    own = lax.broadcasted_iota(jnp.int32, (ATOMS, 256), 1) // NH == lax.broadcasted_iota(jnp.int32, (ATOMS, 256), 0)
-    exp_ref[b] = mm(jnp.where(own, row, 0.0).astype(BF16), rep_ref[...])
+def atom_of_lane():
+    lane = lax.broadcasted_iota(jnp.int32, (ATOMS, 256), 1)
+    return lane // NH == lax.broadcasted_iota(jnp.int32, (ATOMS, 256), 0)
+
+
+def expand_coef(row, rep):
+    return mm(jnp.where(atom_of_lane(), row, 0.0).astype(BF16), rep)
 
 
 def kx_of_rows(glist_ref):
@@ -163,13 +168,18 @@
 
 def augment(first, second, glist_ref, qs_ref, exp_ref, choose_ref, phase_ref, yzt_ref, faug_ref):
     mixed = jnp.concatenate(
-        [exp_ref[i][:, :LM] * exp_ref[j][:, LM:] * choose_ref[...] for i, j in zip(first, second)], axis=0
+        [
+            (exp_ref[i][:, :LM] * exp_ref[j][:, LM:] + exp_ref[j][:, :LM] * exp_ref[i][:, LM:])
+            * (0.5 * choose_ref[...])
+            for i, j in zip(first, second)
+        ],
+        axis=0,
     )
     hi, lo = split(mixed)
     rows = []
     zs = []
     for c in range(2):
-        qh, ql = split(qs_ref[c])
+        qh, ql = qs_ref[2 * c], qs_ref[2 * c + 1]
         zs.append(mm(hi, qh) + mm(lo, qh) + mm(hi, ql))
     z_re, z_im = zs
     for t in range(SLOTS):
@@ -202,7 +212,7 @@
             lhs_ref[at : at + KR, LG:] = im
     rows = NG6 * n * KR
     hi, lo = split(lhs_ref[:rows, :])
-    f = mm(hi, tabs["wfh"][...]) + mm(lo, tabs["wfh"][...]) + mm(hi, tabs["wfl"][...])
+    f = mm(hi, tabs["dft"][0]) + mm(lo, tabs["dft"][0]) + mm(hi, tabs["dft"][1])
     for q in range(NG6):
         kern = tabs["kern"][q * KR : (q + 1) * KR, :]
         for m, t in enumerate(slots):
@@ -215,7 +225,7 @@
                 lhs_ref[at : at + KA, c * LG : (c + 1) * LG] = low
                 lhs_ref[at + KA : at + KR, c * LG : (c + 1) * LG] = w[KA:] * kern[KA:]
     hi, lo = split(lhs_ref[:rows, :])
-    f = mm(hi, tabs["wih"][...]) + mm(lo, tabs["wih"][...]) + mm(hi, tabs["wil"][...])
+    f = mm(hi, tabs["dft"][2]) + mm(lo, tabs["dft"][2]) + mm(hi, tabs["dft"][3])
     for m, t in enumerate(slots):
         v = []
         for q in range(NG6):
@@ -235,7 +245,7 @@
         acc_ref[j] += pot * band_ref[i].astype(F32)[:XO] * twice
 
 
-def slopes(slots, first, second, glist_ref, qs_ref, exp_ref, choose_ref, phase_ref, yzt_ref, wst_ref, pacc_ref):
+def slopes(special, first, second, glist_ref, qs_ref, exp_ref, choose_ref, phase_ref, yzt_ref, wst_ref, pacc_ref):
     hi, lo = split(wst_ref[...])
     picked = mm(hi, yzt_ref[...]) + mm(lo, yzt_ref[...])
     picked = jnp.where(kx_of_rows(glist_ref), picked, 0.0)
@@ -249,81 +259,207 @@
     total = None
     for c, cross in enumerate((re_rows, im_rows)):
         ch, cl = split(jnp.concatenate(cross, axis=0))
-        qh, ql = split(qs_ref[c])
+        qh, ql = qs_ref[2 * c], qs_ref[2 * c + 1]
         part = mm_nt(ch, qh) + mm_nt(cl, qh) + mm_nt(ch, ql)
         total = part if total is None else total + part
-    total = total * (2.0 * AUG / N**3)
+    total = total * (AUG / N**3)
     for t in range(SLOTS):
         slope = total[t * ATOMS : (t + 1) * ATOMS] * choose_ref[...]
+        slope = jnp.concatenate([slope, slope], axis=1)
+        if t == 4:
+            slope = slope * jnp.where(special, 1.0, 0.0)
         i, j = first[t], second[t]
-
-        def give(slope=slope, i=i, j=j):
-            pacc_ref[i] += slope * exp_ref[j][:, LM:]
-            twice = jnp.where(jnp.int32(i) == jnp.int32(j), 0.0, 1.0)
-            pacc_ref[j] += slope * exp_ref[i][:, LM:] * twice
-
-        if t in slots:
-            give()
-        else:
-            pl.when(slots[t])(give)
-
-
-def coef_rows(pacc_ref, rsum_ref):
-    own = lax.broadcasted_iota(jnp.int32, (ATOMS, 256), 1) // NH == lax.broadcasted_iota(jnp.int32, (ATOMS, 256), 0)
-    out = []
-    for b in range(4):
-        hi, lo = split(pacc_ref[b])
-        full = mm(hi, rsum_ref[...]) + mm(lo, rsum_ref[...])
-        out.append(jnp.sum(jnp.where(own, full, 0.0), axis=0, keepdims=True))
-    return out
-
-
-def local_kernel(*refs):
+        swap = lambda b: jnp.concatenate([exp_ref[b][:, LM:], exp_ref[b][:, :LM]], axis=1)
+        twice = jnp.where(jnp.int32(i) == jnp.int32(j), 0.0, 1.0)
+        pacc_ref[i] += slope * swap(j)
+        pacc_ref[j] += slope * swap(i) * twice
+
+
+def coef_row(pacc, rsum):
+    hi, lo = split(pacc)
+    full = mm(hi, rsum) + mm(lo, rsum)
+    return jnp.sum(jnp.where(atom_of_lane(), full, 0.0), axis=0, keepdims=True)
+
+
+def pack_tail(rows):
+    return jnp.concatenate([rows[:, TAIL * j : TAIL * (j + 1)] for j in range(4)], axis=0)
+
+
+def unpack_tail(tail):
+    rows = jnp.concatenate([tail[4 * j : 4 * (j + 1)] for j in range(4)], axis=1)
+    return jnp.concatenate([rows, jnp.zeros((12, LANES), F32)], axis=0)
+
+
+def columns(total, c):
+    start = CHUNK * c
+    parts = []
+    while start < CHUNK * (c + 1):
+        g, at = divmod(start, 216)
+        end = min(216 * (g + 1), CHUNK * (c + 1))
+        parts.append(total[:, g * LG + at : g * LG + at + end - start])
+        start = end
+    return parts[0] if len(parts) == 1 else jnp.concatenate(parts, axis=1)
+
+
+def pack_chunk(total, proj, c):
+    part = columns(total, c)
+    coefs = jnp.concatenate([proj[:, 32 * c : 32 * (c + 1)], jnp.zeros((1, 96), F32)], axis=1)
+    main = jnp.concatenate([part[:N, :128], coefs, jnp.zeros((3, 128), F32)], axis=0)
+    rest = part[:, 128:]
+    last = jnp.concatenate([rest[32:40], jnp.zeros((8, 34), F32)], axis=0)
+    rest = jnp.concatenate([rest[:16], rest[16:32], last, jnp.zeros((16, 26), F32)], axis=1)
+    return jnp.concatenate([main, rest], axis=0)
+
+
+def kernel(*refs):
     nt = len(TABLE_NAMES)
-    (meta_ref, band_ref, coef_ref, qs_ref, species_ref, positions_ref, glist_ref) = refs[:7]
-    tabs = dict(zip(TABLE_NAMES, refs[7 : 7 + nt]))
-    acc_ref = refs[7 + nt]
-    (yzt_ref, phase_ref, choose_ref, exp_ref, faug_ref, wst_ref, lhs_ref, pacc_ref) = refs[8 + nt :]
-    special = meta_ref[0] == 1
-    x = meta_ref[1]
+    bands_ref, coef_ref, q_hbm, species_ref, positions_ref, glist_ref = refs[:6]
+    tables_hbm = refs[6 : 6 + nt]
+    out_ref, proj_ref = refs[6 + nt : 8 + nt]
+    scratch = refs[8 + nt :]
+    tabs = dict(zip(TABLE_NAMES, scratch[:nt]))
+    (band_ref, tail_ref, q_ref, qs_ref, yzt_ref, phase_ref, choose_ref, exp_ref, faug_ref, wst_ref, lhs_ref, pacc_ref,
+     acc_ref, got_ref, pgive_ref, pgot_ref, chunk_ref, chunks_ref,
+     table_sem, tail_send, tail_recv, band_send, band_recv, sum_send, sum_recv, coef_send, coef_recv,
+     chunk_send, chunk_recv) = scratch[nt:]
+    row, col = lax.axis_index("row"), lax.axis_index("col")
+    group, core = row // 2, row % 2
+    offset = (2 * col + core + 1) * (1 - 2 * core)
+    other_offset = (2 * col + 2 - core) * (2 * core - 1)
+    at = lambda g, k: (((g + 64) % 32) * 2 + k, col)
+    sibling = at(group, 1 - core)
+    ahead, ahead_other = at(group + offset, core), at(group + offset, 1 - core)
+    behind, behind_other = at(group - offset, core), at(group - other_offset, 1 - core)
+    peers = [(row, (col + step) % 8) for step in range(1, 8)]
+    mesh_id = pl.DeviceIdType.MESH
+
+    barrier = pltpu.get_barrier_semaphore()
+    partners = [sibling, ahead, ahead_other, behind, behind_other] + peers
+    for partner in partners:
+        pl.semaphore_signal(barrier, inc=1, device_id=partner, device_id_type=mesh_id)
+
+    loads = [
+        pltpu.make_async_copy(src, dst, table_sem.at[n])
+        for n, (src, dst) in enumerate(zip((*tables_hbm, q_hbm), (*scratch[:nt], q_ref)))
+    ]
+    for load in loads:
+        load.start()
+
+    def send(src, dst, to, sems, recvs, n):
+        copy = pltpu.make_async_remote_copy(
+            src_ref=src, dst_ref=dst, send_sem=sems.at[n], recv_sem=recvs.at[n], device_id=to, device_id_type=mesh_id
+        )
+        copy.start()
+        return copy
+
+    field = bands_ref[0].astype(F32)
+    zero = jnp.zeros((N, LG - 216), F32)
+    field = jnp.concatenate(
+        [piece for g in range(NG6) for piece in (field[:, 216 * g : 216 * (g + 1)], zero)], axis=1
+    )
+    band_ref[0, 0:32, :] = field[:32].astype(BF16)
+    tail = pack_tail(field[32:36])
+    coef_rows = jnp.concatenate([coef_ref[...].astype(F32), jnp.zeros((1, TAIL - 256), F32)], axis=1)
+    tail = jnp.concatenate([tail, coef_rows, jnp.zeros((15, TAIL), F32)], axis=0)
+    tail_ref[0] = tail.astype(BF16)
+
+    pl.semaphore_wait(barrier, len(partners))
+    sends = []
+    targets = (behind, behind_other, sibling)
+    slots = (2, 3, 1)
+    tails = [send(tail_ref.at[0], tail_ref.at[b], to, tail_send, tail_recv, b - 1) for b, to in zip(slots, targets)]
+    fields = [
+        send(band_ref.at[0, pl.ds(0, 32)], band_ref.at[b, pl.ds(0, 32)], to, band_send, band_recv, b - 1)
+        for b, to in zip(slots, targets)
+    ]
+    sends += tails + fields
+
+    special = jnp.logical_and(core == 1, col == 7)
+    x = group // 16
     setup_lists(glist_ref, positions_ref, species_ref, yzt_ref, phase_ref, choose_ref)
-    for b in range(4):
-        expand_coef(coef_ref, b, tabs["rep"], exp_ref)
-    first, second = pair_indices(special, x)
     acc_ref[...] = jnp.zeros_like(acc_ref)
     pacc_ref[...] = jnp.zeros_like(pacc_ref)
     wst_ref[...] = jnp.zeros_like(wst_ref)
+    for load in loads:
+        load.wait()
+    for c in range(2):
+        for s in range(NSPEC):
+            hi, lo = split(q_ref[c, s])
+            qs_ref[2 * c, s * 64 : (s + 1) * 64] = hi
+            qs_ref[2 * c + 1, s * 64 : (s + 1) * 64] = lo
+    for b in range(4):
+        if b:
+            tails[slots.index(b)].wait_recv()
+        tail = tail_ref[b].astype(F32)
+        band_ref[b, 32:48, :] = unpack_tail(tail[:16]).astype(BF16)
+        exp_ref[b] = expand_coef(tail[16:17, :256], tabs["rep"][...])
+    first, second = pair_indices(special, x)
     augment(first, second, glist_ref, qs_ref, exp_ref, choose_ref, phase_ref, yzt_ref, faug_ref)
-    run = functools.partial(pairs, first=first, second=second, band_ref=band_ref, faug_ref=faug_ref,
-                            wst_ref=wst_ref, acc_ref=acc_ref, lhs_ref=lhs_ref, tabs=tabs)
+    run = functools.partial(
+        pairs, first=first, second=second, band_ref=band_ref, faug_ref=faug_ref, wst_ref=wst_ref, acc_ref=acc_ref,
+        lhs_ref=lhs_ref, tabs=tabs,
+    )
+    fields[2].wait_recv()
+    fields[0].wait_recv()
     run((0, 1))
+    sums = [send(acc_ref.at[2], got_ref.at[0], ahead, sum_send, sum_recv, 0)]
+    fields[1].wait_recv()
     run((2, 3))
+    sums.append(send(acc_ref.at[3], got_ref.at[1], ahead_other, sum_send, sum_recv, 1))
+    sums.append(send(acc_ref.at[1], got_ref.at[2], sibling, sum_send, sum_recv, 2))
     pl.when(special)(lambda: run((4,)))
-    slopes(SlotSet(special), first, second, glist_ref, qs_ref,
-           exp_ref, choose_ref, phase_ref, yzt_ref, wst_ref, pacc_ref)
-    for b, row in enumerate(coef_rows(pacc_ref, tabs["rsum"])):
-        acc_ref[b, N : N + 1, :LG] = row
-
-
-class SlotSet:
-    def __init__(self, special):
-        self.special = special
-
-    def __contains__(self, t):
-        return t < 4
-
-    def __getitem__(self, t):
-        return self.special
-
-
-def local_call(meta, bands4, coefs4, qs, species, positions, glist):
+    slopes(special, first, second, glist_ref, qs_ref, exp_ref, choose_ref, phase_ref, yzt_ref, wst_ref, pacc_ref)
+    for n, b in enumerate((2, 3, 1)):
+        pgive_ref[n] = jnp.broadcast_to(coef_row(pacc_ref[b], tabs["rsum"][...]), (8, 256))
+    coefs = [
+        send(pgive_ref.at[n], pgot_ref.at[n], to, coef_send, coef_recv, n)
+        for n, to in enumerate((ahead, ahead_other, sibling))
+    ]
+    sends += sums + coefs
+    proj = coef_row(pacc_ref[0], tabs["rsum"][...])
+    total = acc_ref[0]
+    for n in (2, 0, 1):
+        sums[n].wait_recv()
+        total = total + got_ref[n]
+    for n in (2, 0, 1):
+        coefs[n].wait_recv()
+        proj = proj + pgot_ref[n, 0:1, :]
+    for c in range(8):
+        chunk_ref[c] = pack_chunk(total, proj, c)
+    chunks = []
+    for step in range(1, 8):
+        to = (col + step) % 8
+        chunks.append(send(chunk_ref.at[to], chunks_ref.at[step - 1], (row, to), chunk_send, chunk_recv, step - 1))
+    whole = chunk_ref[col]
+    for n, copy in enumerate(chunks):
+        copy.wait_recv()
+        whole = whole + chunks_ref[n]
+    whole = whole * -0.5
+    out_ref[0, :, 0:128] = whole[:N]
+    out_ref[0, 0:16, 128:CHUNK] = whole[40:56, 0:34]
+    out_ref[0, 16:32, 128:CHUNK] = whole[40:56, 34:68]
+    out_ref[0, 32:36, 128:CHUNK] = whole[40:44, 68:102]
+    proj_ref[...] = whole[N : N + 1, 0:32]
+    for copy in sends + chunks:
+        copy.wait_send()
+
+
+def on_device(bands, projections, qfunc, species, positions, glist):
     vm = pl.BlockSpec(memory_space=pltpu.VMEM)
+    hbm = pl.BlockSpec(memory_space=pl.ANY)
+    tables = [jnp.asarray(TABLES[name]) for name in TABLE_NAMES]
+    dma = pltpu.SemaphoreType.DMA
     return pl.pallas_call(
-        local_kernel,
-        out_shape=jax.ShapeDtypeStruct((4, XO, LANES), F32),
-        in_specs=[pl.BlockSpec(memory_space=pltpu.SMEM)] + [vm] * (6 + len(TABLE_NAMES)),
-        out_specs=vm,
+        kernel,
+        out_shape=(jax.ShapeDtypeStruct((1, N, CHUNK), F32), jax.ShapeDtypeStruct((1, 32), F32)),
+        in_specs=[vm, vm, hbm, vm, vm, vm] + [hbm] * len(tables),
+        out_specs=(vm, vm),
         scratch_shapes=[
+            *[pltpu.VMEM(t.shape, t.dtype) for t in tables],
+            pltpu.VMEM((4, XB, LANES), BF16),
+            pltpu.VMEM((4, 32, TAIL), BF16),
+            pltpu.VMEM((2, NSPEC, NH * NH, NLIST), F32),
+            pltpu.VMEM((4, LM, NLIST), BF16),
             pltpu.VMEM((LANES, NLIST), BF16),
             pltpu.VMEM((2, ATOMS, NLIST), F32),
             pltpu.VMEM((ATOMS, LM), F32),
@@ -331,47 +467,21 @@
             pltpu.VMEM((SLOTS * 2 * KA, LANES), F32),
             pltpu.VMEM((SLOTS * 2 * KA, LANES), F32),
             pltpu.VMEM((2 * NG6 * KR, 2 * LG), F32),
-            pltpu.VMEM((4, ATOMS, LM), F32),
+            pltpu.VMEM((4, ATOMS, 2 * LM), F32),
+            pltpu.VMEM((4, XO, LANES), F32),
+            pltpu.VMEM((3, XO, LANES), F32),
+            pltpu.VMEM((3, 8, 256), F32),
+            pltpu.VMEM((3, 8, 256), F32),
+            pltpu.VMEM((8, 56, 128), F32),
+            pltpu.VMEM((7, 56, 128), F32),
+            dma((len(tables) + 1,)),
+            *[dma((3,)) for unused in range(8)],
+            *[dma((7,)) for unused in range(2)],
         ],
-        compiler_params=pltpu.CompilerParams(vmem_limit_bytes=48 * 2**20),
-    )(meta, bands4, coefs4, qs, species.reshape(1, ATOMS), positions, glist.reshape(1, NLIST),
-      *[jnp.asarray(TABLES[name]) for name in TABLE_NAMES])
-
-
-def offset_of(slot):
-    return slot + 1 if slot % 2 == 0 or slot == 15 else 32 - (slot + 1)
-
-
-def on_device(bands, projections, qfunc, species, positions, glist):
-    row, col = lax.axis_index("row"), lax.axis_index("col")
-    group, core = row // 2, row % 2
-    slot = col * 2 + core
-    special = slot == 15
-    x = jnp.where(group >= 16, 1, 0)
-    meta = jnp.stack([special.astype(jnp.int32), x.astype(jnp.int32)])
-    dev = lambda g, c, k: ((g % 32) * 2 + k) * 8 + c
-    ids = [(g, c, k) for g in range(32) for c in range(8) for k in range(2)]
-    sib = [(dev(g, c, k), dev(g, c, 1 - k)) for g, c, k in ids]
-    near = [(dev(g, c, k), dev(g - offset_of(2 * c + k), c, k)) for g, c, k in ids]
-    far = [(dev(g, c, k), dev(g - offset_of(2 * c + 1 - k), c, 1 - k)) for g, c, k in ids]
-    back = [(b, a) for a, b in near]
-    axes = ("row", "col")
-    field = jnp.pad(bands[0].reshape(N, NG6, 216), ((0, XB - N), (0, 0), (0, LG - 216))).reshape(XB, LANES)
-    coef = projections
-    parts = [(field, coef)] + [(lax.ppermute(field, axes, p), lax.ppermute(coef, axes, p)) for p in (sib, near, far)]
-    bands4 = jnp.stack([p[0] for p in parts])
-    coefs4 = jnp.stack([p[1] for p in parts])
-    q5 = qfunc.reshape(2, NSPEC, NH, NH, NLIST)
-    qs = (0.5 * (q5 + jnp.swapaxes(q5, 2, 3))).reshape(2, LM, NLIST)
-    acc = local_call(meta, bands4, coefs4, qs, species, positions, glist)
-    got = lax.ppermute(acc[2:], axes, back)
-    mine = acc[:2] + got
-    total = mine[0] + lax.ppermute(mine[1], axes, sib)
-    grid = total[:N].reshape(N, NG6, LG)[:, :, :216].reshape(N, 8, 162).transpose(1, 0, 2)
-    proj = total[N, :LG].reshape(8, 32)
-    grid = lax.all_to_all(grid, "col", 0, 0, tiled=True)
-    proj = lax.all_to_all(proj, "col", 0, 0, tiled=True)
-    return (-0.5 * jnp.sum(grid.reshape(8, N, 162), axis=0)[None], -0.5 * jnp.sum(proj.reshape(8, 32), axis=0)[None])
+        compiler_params=pltpu.CompilerParams(
+            collective_id=0, has_side_effects=True, vmem_limit_bytes=48 * 2**20
+        ),
+    )(bands, projections, qfunc, species.reshape(1, ATOMS), positions, glist.reshape(1, NLIST), *tables)
 
 
 def solution(mesh):

time: 140 us -> 97.3 us (0.69)
  the two profiles are of different devices: /device:TPU:16 before, /device:TPU:56 now
where the time goes in v1:
time: 97.3 us; the launch traced here: 96.7 us
  Pallas kernels  83.6 us (86%)
  local copies, waits for them, and re-layouts  12.5 us (13%)
    pallas_call x1, Pallas kernels, on_device(): pl.pallas_call(kernel, out_shape=(jax.ShapeDtypeStruct((1, N, CHUNK), F32...  83.6 us
    unnamed x27, local copies, waits for them, and re-layouts  11.8 us

profile of v1, /device:TPU:56, one launch (start us, length us, event | category | flops | bytes accessed | tf_op | source)
XLA Modules:
  0.0 96.7 jit_solution(11184986682673877021)
XLA Ops:
  0.6 0.0 copy-start
  0.6 1.6 %copy-done = bf16[4,512,512]{2,1,0:T(8,128)(2,1)S(1)} copy-done((bf16[4,512,512]{2,1,0:T(8,128)(2,1)S(1)}, bf16[4,512,512]{2,1,0:T(8,128)(2,1)}, u32[]{:S(2)}) %copy-start) | copy-done | bytes 2097176
  2.2 0.0 copy-start.1
  2.2 1.2 %copy-done.1 = f32[2,2,64,1024]{3,2,1,0:T(8,128)S(1)} copy-done((f32[2,2,64,1024]{3,2,1,0:T(8,128)S(1)}, f32[2,2,64,1024]{3,2,1,0:T(8,128)}, u32[]{:S(2)}) %copy-start.1) | copy-done | bytes 1048600
  3.5 0.0 copy-start.2
  3.5 0.9 copy-done.2
  4.4 0.0 copy-start.3
  4.4 0.9 copy-done.3
  5.3 0.0 copy-start.4
  5.3 0.9 copy-done.4
  6.2 0.0 copy-start.5
  6.2 0.9 copy-done.5
  7.1 0.0 copy-start.6
  7.1 0.7 copy-done.6
  7.8 0.0 copy-start.7
  7.8 0.7 copy-done.7
  8.5 0.0 copy-start.8
  8.5 0.7 copy-done.8
  9.3 0.0 copy-start.9
  9.3 0.7 copy-done.9
  9.9 0.0 copy-start.10
  9.9 0.7 copy-done.10
  10.6 0.0 copy-start.11
  10.6 0.7 copy-done.11
  11.3 0.0 copy-start.12
  11.3 0.7 copy-done.12
  12.0 83.6 %shard_map.140 = (f32[1,36,162]{2,1,0:T(8,128)S(1)}, f32[1,32]{1,0:T(1,128)S(1)}) custom-call(bf16[1,36,1296]{2,1,0:T(8,128)(2,1)S(1)} %copy-done.5, bf16[1,256]{1,0:T(2,128)(2,1)S(1)} %copy-done.11, f32[2,2,64,1024]{3,2,1,0:T(8,128)S(1)} %copy-done.1, s32[1,32]{1,0:T(1,128)S(1)} %bitcast.3, f32[3,32]{1,0:T(4,128)S(1)} %copy-done.10, s32[1,1024]{1,0:T(1,128)S(1)} %bitcast.2, ...), custom_call_target="tpu_custom_call" | custom-call | tf_op jit(solution)/shard_map/pallas_call | solution.py:452
  95.6 0.7 copy.15
  96.2 0.5 copy.17
Async XLA Ops:
  0.6 1.6 %copy-start = (bf16[4,512,512]{2,1,0:T(8,128)(2,1)S(1)}, bf16[4,512,512]{2,1,0:T(8,128)(2,1)}, u32[]{:S(2)}) copy-start(bf16[4,512,512]{2,1,0:T(8,128)(2,1)} %constant.16.clone.refs_8_) | copy-start | bytes 6291460
  2.2 1.2 %copy-start.1 = (f32[2,2,64,1024]{3,2,1,0:T(8,128)S(1)}, f32[2,2,64,1024]{3,2,1,0:T(8,128)}, u32[]{:S(2)}) copy-start(f32[2,2,64,1024]{3,2,1,0:T(8,128)} %refs_2_.1) | copy-start | bytes 3145732
  3.5 0.9 copy-start.2
  4.4 0.9 copy-start.3
  5.3 0.9 copy-start.4
  6.2 0.9 copy-start.5
  7.1 0.7 copy-start.6
  7.8 0.7 copy-start.7
  8.5 0.7 copy-start.8
  9.3 0.7 copy-start.9
  9.9 0.7 copy-start.10
  10.6 0.7 copy-start.11
  11.3 0.7 copy-start.12

commit v2 on v1

v2 whole, which is shorter than its diff:
```python
import functools
import math

import jax
import jax.numpy as jnp
import ml_dtypes
import numpy as np
from jax import lax
from jax.experimental import pallas as pl
from jax.experimental.pallas import tpu as pltpu
from jax.sharding import PartitionSpec as P

N = 36
NG6 = 6
LG = 256
LOWL = 128
LANES = NG6 * LG
XB = 48
XO = 40
KL = 24
KR = 40
ATOMS, NH, NSPEC, NLIST = 32, 8, 2, 1024
PK = 80
AUG = N**1.5 / (NH * math.sqrt(ATOMS))
STEPS = 4
TAIL = 384
CHUNK = 162
F32, BF16 = jnp.float32, jnp.bfloat16

OFFSETS = [
    *[[(1, j), (-1, (j + 1) % 4), (3, (j + 2) % 4), (-3, (j + 3) % 4)] for j in range(4)],
    *[[(2, j), (-2, 1 ^ j), (2, 2 ^ j), (-2, 3 ^ j)] for j in range(2)],
    *[[(0, j), (4, 1 ^ j), (0, 2 ^ j), (4, 3 ^ j)] for j in range(2)],
]


def split_np(a):
    hi = a.astype(np.float32).astype(ml_dtypes.bfloat16)
    lo = (a - hi.astype(np.float64)).astype(np.float32).astype(ml_dtypes.bfloat16)
    return hi, lo


def row_of(pair, kx):
    return 11 * pair + kx if kx <= 10 else KL + 8 * pair + kx - 11


def make_tables():
    k = np.arange(19)[:, None]
    x = np.arange(N)[None, :]
    ang = 2 * np.pi * (k * x % N) / N
    weight = np.where((k == 0) | (k == N // 2), 1.0, 2.0) / N**3
    parts = (np.cos(ang), -np.sin(ang))
    bf = ml_dtypes.bfloat16
    fwd = np.zeros((4 * KR, 4 * XB), bf)
    inv = np.zeros((2 * XO, 6 * KR), bf)
    for pair in range(2):
        for c, part in enumerate(parts):
            fh, fl = split_np(part)
            ih, il = split_np(weight * part)
            for kx in range(19):
                r = c * KR + row_of(pair, kx)
                fwd[r, 96 * pair : 96 * pair + N] = fh[kx]
                fwd[r, 96 * pair + XB : 96 * pair + XB + N] = fh[kx]
                fwd[2 * KR + r, 96 * pair : 96 * pair + N] = fl[kx]
                for b, values in enumerate((ih, ih, il)):
                    inv[XO * pair : XO * pair + N, 2 * KR * b + r] = values[kx]
    r_of = np.repeat(np.arange(6), N)
    z_of = np.tile(np.arange(N), 6)
    near = [(s, kz) for s in (0, 1, 4, 5) for kz in (*range(11), *range(26, 36))]
    order = near + [(s, kz) for s in range(6) for kz in range(N) if (s, kz) not in near]
    s_of = np.array([p[0] for p in order])
    k_of = np.array([p[1] for p in order])
    ang = 2 * np.pi * ((6 * r_of[:, None] * s_of[None, :] + z_of[:, None] * k_of[None, :]) % N) / N
    c = np.zeros((LG, LG))
    s = np.zeros((LG, LG))
    c[:216, :216] = np.cos(ang)
    s[:216, :216] = np.sin(ang)

    def stacked(w):
        hi, lo = split_np(w)
        return np.concatenate([hi, hi, lo], axis=0)

    dft = np.stack([stacked(w) for w in (c, c - s, c + s, c.T, (c + s).T, (c - s).T)])
    tw = np.zeros((16, LG), np.float32)
    for q in range(6):
        a = 2 * np.pi * (r_of * q % N) / N
        tw[q, :216] = np.cos(a)
        tw[8 + q, :216] = -np.sin(a)
    signed = lambda v: np.where(v > N // 2, v - N, v)
    kern = np.zeros((NG6 * KR, LG), np.float32)
    for q in range(6):
        for pair in range(2):
            for kx in range(19):
                n2 = kx**2 + signed(q + 6 * s_of) ** 2 + signed(k_of) ** 2
                kern[q * KR + row_of(pair, kx), :216] = np.where(n2 > 0, N**1.5 / 4 / np.maximum(n2, 1), 0)
    packed = [(s, l, m) for s in range(NSPEC) for l in range(NH) for m in range(l, NH)]
    sel = np.zeros((PK, NSPEC * NH * NH), np.float32)
    rep = np.zeros((256, 768), np.float32)
    rsum = np.zeros((256, 256), np.float32)
    weight = np.zeros((NSPEC, LG), np.float32)
    kk = np.arange(256) % NH
    for p, (s, l, m) in enumerate(packed):
        sel[p, s * 64 + l * 8 + m] += 0.5
        sel[p, s * 64 + m * 8 + l] += 0.5
        for b in range(3):
            rep[kk == l, PK * b + p] = 1
            rep[kk == m, LG + PK * b + p] = 1
            weight[s, PK * b + p] = 0.5 if l == m else 1.0
        rep[kk == m, 2 * LG + p] = 1
        rsum[p, kk == l] = 1
        if l != m:
            rep[kk == l, 2 * LG + PK + p] = 1
            rsum[PK + p, kk == m] = 1
    return dict(
        fwd=fwd, inv=inv, dft=dft, tw=tw, kern=kern, sel=sel.astype(bf), rep=rep.astype(bf), rsum=rsum.astype(bf),
        weight=np.concatenate([weight, np.zeros((6, LG), np.float32)]),
    )


TABLES = make_tables()
TABLE_NAMES = ("fwd", "inv", "dft", "tw", "kern", "sel", "rep", "rsum", "weight")


def split(a):
    hi = a.astype(BF16)
    return hi, (a - hi.astype(F32)).astype(BF16)


def mm(a, b):
    return jnp.dot(a, b, preferred_element_type=F32)


def mm_nt(a, b):
    return lax.dot_general(a, b, (((1,), (1,)), ((), ())), preferred_element_type=F32)


def dft3(a, b, c, sign):
    h = math.sqrt(3.0) / 2
    sr, si = b[0] + c[0], b[1] + c[1]
    dr, di = (b[0] - c[0]) * h, (b[1] - c[1]) * h
    tr, ti = a[0] - 0.5 * sr, a[1] - 0.5 * si
    zero = (a[0] + sr, a[1] + si)
    minus = (tr + di, ti - dr)
    plus = (tr - di, ti + dr)
    return (zero, minus, plus) if sign < 0 else (zero, plus, minus)


def dft6(v, sign):
    add = lambda p, q: (p[0] + q[0], p[1] + q[1])
    sub = lambda p, q: (p[0] - q[0], p[1] - q[1])
    e = dft3(add(v[0], v[3]), add(v[1], v[4]), add(v[2], v[5]), sign)
    o = dft3(sub(v[0], v[3]), sub(v[4], v[1]), sub(v[2], v[5]), sign)
    return [e[0], o[2], e[1], o[0], e[2], o[1]]


def mm3(x, w):
    hi, lo = split(x)
    return mm(jnp.concatenate([hi, lo, hi], axis=1), w)


def atom_of_lane():
    lane = lax.broadcasted_iota(jnp.int32, (ATOMS, 256), 1)
    return lane // NH == lax.broadcasted_iota(jnp.int32, (ATOMS, 256), 0)


def setup_lists(glist_ref, positions_ref, species_ref, weight_ref, yzt_ref, phase_ref, choose_ref):
    g = glist_ref[...]
    kx = g // (N * N)
    ky = g // N % N
    kz = g % N
    s = ky // 6
    where = (ky % 6) * LOWL + jnp.where(s < 2, s, s - 2) * 21 + jnp.where(kz <= 10, kz, kz - 15)
    step = 256
    for base in range(0, NG6 * LOWL, step):
        rows = lax.broadcasted_iota(jnp.int32, (step, NLIST), 0) + base
        yzt_ref[base : base + step, :] = jnp.where(rows == where, 1.0, 0.0).astype(BF16)
    sg = lambda v: jnp.where(v > N // 2, v - N, v).astype(F32)
    eye = lax.broadcasted_iota(jnp.int32, (ATOMS, ATOMS), 0) == lax.broadcasted_iota(jnp.int32, (ATOMS, ATOMS), 1)
    column = lambda row: jnp.sum(jnp.where(eye, row, 0.0), axis=1, keepdims=True)
    turns = (
        column(positions_ref[0:1, :]) * kx.astype(F32)
        + column(positions_ref[1:2, :]) * sg(ky)
        + column(positions_ref[2:3, :]) * sg(kz)
    )
    theta = (turns - jnp.floor(turns)) * (2.0 * math.pi)
    phase_ref[0] = jnp.cos(theta)
    phase_ref[1] = -jnp.sin(theta)
    spec = column(species_ref[...].astype(F32))
    choose = jnp.zeros((ATOMS, LG), F32)
    for s in range(NSPEC):
        choose = choose + jnp.where(spec == float(s), 1.0, 0.0) * weight_ref[s : s + 1, :]
    choose_ref[...] = choose


def kx_rows(glist_ref):
    kx = glist_ref[...] // (N * N)
    rows = lax.broadcasted_iota(jnp.int32, (KL, NLIST), 0)
    return rows == kx, rows == kx + 11


def augment(glist_ref, qz_ref, exp_ref, choose_ref, phase_ref, yzt_ref, faug_ref):
    lane = lax.broadcasted_iota(jnp.int32, (ATOMS, LG), 1)
    middle = jnp.logical_and(lane >= PK, lane < 2 * PK)
    mixed = []
    for t in range(STEPS):
        for i in range(2):
            a, b = exp_ref[i], exp_ref[2 + t]
            full = (a[:, :LG] * b[:, LG : 2 * LG] + b[:, :LG] * a[:, LG : 2 * LG]) * choose_ref[...]
            hi = full.astype(BF16).astype(F32)
            mixed.append(jnp.where(middle, full - hi, hi).astype(BF16)[:, : 3 * PK])
    mixed = jnp.concatenate(mixed, axis=0)
    z_re = mm(mixed, qz_ref[:, :NLIST])
    z_im = mm(mixed, qz_ref[:, NLIST:])
    first, second = kx_rows(glist_ref)
    spread = []
    for t in range(STEPS):
        re, im = [], []
        for i in range(2):
            at = (2 * t + i) * ATOMS
            zr, zi = z_re[at : at + ATOMS], z_im[at : at + ATOMS]
            re.append(jnp.sum(phase_ref[0] * zr - phase_ref[1] * zi, axis=0, keepdims=True) * AUG)
            im.append(jnp.sum(phase_ref[0] * zi + phase_ref[1] * zr, axis=0, keepdims=True) * AUG)
        for rows in (re, im):
            spread.append(jnp.where(first, rows[0], jnp.where(second, rows[1], 0.0)))
    hi, lo = split(jnp.concatenate(spread, axis=0))
    both = jnp.concatenate([hi, lo], axis=0)
    for base in range(0, NG6 * LOWL, LG):
        part = mm_nt(both, yzt_ref[base : base + LG, :])
        part = part[:192] + part[192:]
        for t in range(STEPS):
            faug_ref[t, :, base : base + LG] = part[48 * t : 48 * (t + 1)]


def batch(t, band_ref, faug_ref, wst_ref, acc_ref, tabs):
    other = band_ref[2 + t].astype(F32)
    halves = []
    for i in range(2):
        halves += split(band_ref[i].astype(F32) * other)
    out = mm(tabs["fwd"][...], jnp.concatenate(halves, axis=0))
    spec = out[: 2 * KR] + out[2 * KR :]
    v = [(spec[:KR, g * LG : (g + 1) * LG], spec[KR:, g * LG : (g + 1) * LG]) for g in range(NG6)]
    re_rows, im_rows = [], []
    for q, (re, im) in enumerate(dft6(v, -1)):
        if q:
            cr, ci = tabs["tw"][q : q + 1, :], tabs["tw"][8 + q : 9 + q, :]
            re, im = re * cr - im * ci, re * ci + im * cr
        re_rows.append(re)
        im_rows.append(im)
    re, im = jnp.concatenate(re_rows, axis=0), jnp.concatenate(im_rows, axis=0)
    both = mm3(re + im, tabs["dft"][0])
    f = (both - mm3(im, tabs["dft"][1]), both - mm3(re, tabs["dft"][2]))
    w = []
    for c in range(2):
        rows = []
        for q in range(NG6):
            block = f[c][q * KR : (q + 1) * KR]
            kern = tabs["kern"][q * KR : (q + 1) * KR, :]
            low = (block[:KL, :LOWL] + faug_ref[t, c * KL : (c + 1) * KL, q * LOWL : (q + 1) * LOWL]) * kern[:KL, :LOWL]
            wst_ref[t, c * KL : (c + 1) * KL, q * LOWL : (q + 1) * LOWL] = low
            rows.append(jnp.concatenate([low, block[:KL, LOWL:] * kern[:KL, LOWL:]], axis=1))
            rows.append(block[KL:] * kern[KL:])
        w.append(jnp.concatenate(rows, axis=0))
    both = mm3(w[0] + w[1], tabs["dft"][3])
    re, im = both - mm3(w[1], tabs["dft"][4]), both - mm3(w[0], tabs["dft"][5])
    v = []
    for q in range(NG6):
        a, b = re[q * KR : (q + 1) * KR], im[q * KR : (q + 1) * KR]
        if q:
            cr, ci = tabs["tw"][q : q + 1, :], tabs["tw"][8 + q : 9 + q, :]
            a, b = a * cr + b * ci, b * cr - a * ci
        v.append((a, b))
    v = dft6(v, 1)
    w = jnp.concatenate([jnp.concatenate([p[0], p[1]], axis=0) for p in v], axis=1)
    hi, lo = split(w)
    pot = mm(tabs["inv"][...], jnp.concatenate([hi, lo, hi], axis=0))
    acc_ref[0] += pot[:XO] * other[:XO]
    acc_ref[1] += pot[XO:] * other[:XO]


def slopes(glist_ref, qz_ref, exp_ref, choose_ref, phase_ref, yzt_ref, wst_ref):
    hi, lo = split(wst_ref[...].reshape(STEPS * 2 * KL, NG6 * LOWL))
    picked = mm(jnp.concatenate([hi, lo], axis=0), yzt_ref[...])
    picked = picked[:192] + picked[192:]
    first, second = kx_rows(glist_ref)
    cross = []
    for t in range(STEPS):
        for mask in (first, second):
            at = t * 2 * KL
            wr = jnp.sum(jnp.where(mask, picked[at : at + KL], 0.0), axis=0, keepdims=True)
            wi = jnp.sum(jnp.where(mask, picked[at + KL : at + 2 * KL], 0.0), axis=0, keepdims=True)
            re = wr * phase_ref[0] + wi * phase_ref[1]
            im = wi * phase_ref[0] - wr * phase_ref[1]
            cross.append(jnp.concatenate([re, im], axis=1))
    hi, lo = split(jnp.concatenate(cross, axis=0))
    full = mm_nt(jnp.concatenate([hi, lo], axis=0), qz_ref[...])
    high, low = full[:256], full[256:]
    rest = high[:, 2 * PK :]
    slope = (high[:, : 2 * PK] + low[:, : 2 * PK] + jnp.concatenate([rest, rest], axis=1)) * (2.0 * AUG / N**3)
    slope = jnp.concatenate([slope, jnp.zeros((256, LG - 2 * PK), F32)], axis=1)
    chosen = jnp.where(choose_ref[...] > 0.0, 1.0, 0.0)
    sums = []
    for i in range(2):
        total = jnp.zeros((ATOMS, LG), F32)
        for t in range(STEPS):
            at = (2 * t + i) * ATOMS
            total = total + slope[at : at + ATOMS] * exp_ref[2 + t][:, 2 * LG :]
        sums.append(total * chosen)
    return sums


def coef_row(packed, rsum):
    hi, lo = split(packed)
    full = mm(hi, rsum) + mm(lo, rsum)
    return jnp.sum(jnp.where(atom_of_lane(), full, 0.0), axis=0, keepdims=True)


def pack_tail(rows):
    return jnp.concatenate([rows[:, TAIL * j : TAIL * (j + 1)] for j in range(4)], axis=0)


def unpack_tail(tail):
    rows = jnp.concatenate([tail[4 * j : 4 * (j + 1)] for j in range(4)], axis=1)
    return jnp.concatenate([rows, jnp.zeros((12, LANES), F32)], axis=0)


def columns(total, c):
    start = CHUNK * c
    parts = []
    while start < CHUNK * (c + 1):
        g, at = divmod(start, 216)
        end = min(216 * (g + 1), CHUNK * (c + 1))
        parts.append(total[:, g * LG + at : g * LG + at + end - start])
        start = end
    return parts[0] if len(parts) == 1 else jnp.concatenate(parts, axis=1)


def pack_chunk(total, c):
    part = columns(total, c)
    main = part[:, :128]
    rest = part[:, 128:]
    last = jnp.concatenate([rest[32:40], jnp.zeros((8, 34), F32)], axis=0)
    rest = jnp.concatenate([rest[:16], rest[16:32], last, jnp.zeros((16, 26), F32)], axis=1)
    return jnp.concatenate([main, rest], axis=0)


def kernel(*refs):
    nt = len(TABLE_NAMES)
    sources = refs[: 6 + nt]
    out_ref, proj_ref = refs[6 + nt : 8 + nt]
    scratch = refs[8 + nt :]
    bands_ref, coef_ref, q_ref, species_ref, positions_ref, glist_ref = scratch[:6]
    tabs = dict(zip(TABLE_NAMES, scratch[6 : 6 + nt]))
    (band_ref, tail_ref, qz_ref, yzt_ref, phase_ref, choose_ref, exp_ref, faug_ref, wst_ref,
     acc_ref, got_ref, pgive_ref, pgot_ref, chunk_ref, chunks_ref,
     load_sem, tail_send, tail_recv, band_send, band_recv, sum_send, sum_recv, coef_send, coef_recv,
     chunk_send, chunk_recv) = scratch[6 + nt :]
    row, col = lax.axis_index("row"), lax.axis_index("col")
    zed, wide, core = row // 8, row // 2 % 4, row % 2

    def pick(values):
        return sum(jnp.where(col == c, v, 0) for c, v in enumerate(values))

    def at(dz, dy, k):
        return (((zed + dz + 16) % 8 * 4 + (wide + dy + 8) % 4) * 2 + k, col)

    sibling = at(0, 0, 1 - core)
    targets, origins = [], []
    for m in range(4):
        targets.append(at(-pick([o[m][0] for o in OFFSETS]), -pick([o[m][1] for o in OFFSETS]), m % 2))
    for n in range(2):
        dz, dy = (
            pick([o[2 * n][e] for o in OFFSETS]) * (1 - core) + pick([o[2 * n + 1][e] for o in OFFSETS]) * core
            for e in range(2)
        )
        origins += [at(dz, dy, k) for k in range(2)]
    home = jnp.logical_and(col == 6, core == 0)
    away = jnp.logical_not(home)
    peers = [(row, (col + step) % 8) for step in range(1, 8)]
    cousins = [(sibling[0], (col + step) % 8) for step in range(1, 8)]
    mesh_id = pl.DeviceIdType.MESH

    barrier = pltpu.get_barrier_semaphore()

    def greet(partner):
        pl.semaphore_signal(barrier, inc=1, device_id=partner, device_id_type=mesh_id)

    pl.when(away)(lambda: greet(origins[0]))
    others = origins[1:] + [sibling] + peers + cousins
    for partner in others:
        greet(partner)

    loads = [
        pltpu.make_async_copy(src, dst, load_sem.at[n]) for n, (src, dst) in enumerate(zip(sources, scratch[: 6 + nt]))
    ]
    for load in loads:
        load.start()

    def remote(src, dst, to, sems, recvs, n, m=None):
        return pltpu.make_async_remote_copy(
            src_ref=src, dst_ref=dst, send_sem=sems.at[n], recv_sem=recvs.at[n if m is None else m],
            device_id=to, device_id_type=mesh_id,
        )

    loads[0].wait()
    loads[1].wait()
    field = bands_ref[0].astype(F32)
    zero = jnp.zeros((N, LG - 216), F32)
    field = jnp.concatenate(
        [piece for g in range(NG6) for piece in (field[:, 216 * g : 216 * (g + 1)], zero)], axis=1
    )
    band_ref[0, 0:32, :] = field[:32].astype(BF16)
    tail = pack_tail(field[32:36])
    coef_rows = jnp.concatenate([coef_ref[...].astype(F32), jnp.zeros((1, TAIL - 256), F32)], axis=1)
    tail = jnp.concatenate([tail, coef_rows, jnp.zeros((15, TAIL), F32)], axis=0)
    tail_ref[0] = tail.astype(BF16)

    pl.semaphore_wait(barrier, len(others) + 1 - home.astype(jnp.int32))
    tails = [remote(tail_ref.at[0], tail_ref.at[1], sibling, tail_send, tail_recv, 4)]
    fields = [remote(band_ref.at[0, pl.ds(0, 32)], band_ref.at[1, pl.ds(0, 32)], sibling, band_send, band_recv, 4)]
    for m in range(4):
        t = 2 * (m // 2) + core
        tails.append(remote(tail_ref.at[0], tail_ref.at[2 + t], targets[m], tail_send, tail_recv, m, t))
        fields.append(
            remote(
                band_ref.at[0, pl.ds(0, 32)], band_ref.at[2 + t, pl.ds(0, 32)], targets[m], band_send, band_recv, m, t
            )
        )
    for group in (tails, fields):
        for n, copy in enumerate(group):
            if n == 1:
                pl.when(away)(copy.start)
            else:
                copy.start()

    for load in loads[2:]:
        load.wait()
    setup_lists(glist_ref, positions_ref, species_ref, tabs["weight"], yzt_ref, phase_ref, choose_ref)
    acc_ref[...] = jnp.zeros_like(acc_ref)
    for c in range(2):
        hi, lo = split(q_ref[c].reshape(NSPEC * NH * NH, NLIST))
        packed = mm(tabs["sel"][...], hi) + mm(tabs["sel"][...], lo)
        hi, lo = split(packed)
        qz_ref[:, c * NLIST : (c + 1) * NLIST] = jnp.concatenate([hi, hi, lo], axis=0)

    def arrived(which, ref, recvs, n):
        pltpu.make_async_remote_copy(
            src_ref=which, dst_ref=ref, send_sem=recvs.at[n], recv_sem=recvs.at[n], device_id=sibling,
            device_id_type=mesh_id,
        ).wait_recv()

    def home_tail():
        tail_ref[2] = tail_ref[0]

    pl.when(home)(home_tail)
    for b in range(2 + STEPS):
        if b:
            wait = functools.partial(arrived, tail_ref.at[0], tail_ref.at[b], tail_recv, (b + 3) % 5)
            if b == 2:
                pl.when(away)(wait)
            else:
                wait()
        tail = tail_ref[b].astype(F32)
        band_ref[b, 32:48, :] = unpack_tail(tail[:16]).astype(BF16)
        spread = jnp.where(atom_of_lane(), tail[16:17, :256], 0.0).astype(BF16)
        exp_ref[b] = mm(spread, tabs["rep"][...])
    augment(glist_ref, qz_ref, exp_ref, choose_ref, phase_ref, yzt_ref, faug_ref)

    def home_band():
        band_ref[2, 0:32, :] = band_ref[0, 0:32, :]

    pl.when(home)(home_band)
    arrived(band_ref.at[0, pl.ds(0, 32)], band_ref.at[1, pl.ds(0, 32)], band_recv, 4)

    def step(t, carry):
        wait = lambda: arrived(band_ref.at[0, pl.ds(0, 32)], band_ref.at[2 + t, pl.ds(0, 32)], band_recv, t)
        pl.when(jnp.logical_or(away, t > 0))(wait)
        batch(t, band_ref, faug_ref, wst_ref, acc_ref, tabs)
        return carry

    lax.fori_loop(0, STEPS, step, 0)
    give = remote(acc_ref.at[1], got_ref, sibling, sum_send, sum_recv, 0)
    give.start()
    give.wait_recv()
    total = acc_ref[0] + got_ref[...]
    for c in range(8):
        chunk_ref[c] = pack_chunk(total, c)
    chunks = []
    for n, to in enumerate(peers):
        chunks.append(remote(chunk_ref.at[to[1]], chunks_ref.at[n], to, chunk_send, chunk_recv, n))
        chunks[-1].start()
    sums = slopes(glist_ref, qz_ref, exp_ref, choose_ref, phase_ref, yzt_ref, wst_ref)
    rows = [coef_row(packed, tabs["rsum"][...]) for packed in sums]
    for i in range(2):
        pgive_ref[i] = jnp.broadcast_to(rows[i], (8, 256))
    coefs = []
    for n, to in enumerate(peers + [sibling] + cousins):
        coefs.append(remote(pgive_ref.at[0 if n < 7 else 1], pgot_ref.at[n], to, coef_send, coef_recv, n))
        coefs[-1].start()
    whole = chunk_ref[col]
    for n, copy in enumerate(chunks):
        copy.wait_recv()
        whole = whole + chunks_ref[n]
    whole = whole * -0.5
    out_ref[0, :, 0:128] = whole[:N]
    out_ref[0, 0:16, 128:CHUNK] = whole[40:56, 0:34]
    out_ref[0, 16:32, 128:CHUNK] = whole[40:56, 34:68]
    out_ref[0, 32:36, 128:CHUNK] = whole[40:44, 68:102]
    proj = rows[0]
    for n, copy in enumerate(coefs):
        copy.wait_recv()
        proj = proj + pgot_ref[n, 0:1, :]
    proj_ref[...] = -0.5 * sum(jnp.where(col == c, proj[:, 32 * c : 32 * (c + 1)], 0.0) for c in range(8))
    for group in (tails, fields):
        for n, copy in enumerate(group):
            if n == 1:
                pl.when(away)(copy.wait_send)
            else:
                copy.wait_send()
    for copy in [give] + chunks + coefs:
        copy.wait_send()


def on_device(bands, projections, qfunc, species, positions, glist):
    hbm = pl.BlockSpec(memory_space=pltpu.HBM)
    vm = pl.BlockSpec(memory_space=pltpu.VMEM)
    sources = [bands, projections, qfunc, species.reshape(1, ATOMS), positions, glist.reshape(1, NLIST)]
    sources += [jnp.asarray(TABLES[name]) for name in TABLE_NAMES]
    dma = pltpu.SemaphoreType.DMA
    return pl.pallas_call(
        kernel,
        out_shape=(jax.ShapeDtypeStruct((1, N, CHUNK), F32), jax.ShapeDtypeStruct((1, 32), F32)),
        in_specs=[hbm] * len(sources),
        out_specs=(vm, vm),
        scratch_shapes=[
            *[pltpu.VMEM(t.shape, t.dtype) for t in sources],
            pltpu.VMEM((2 + STEPS, XB, LANES), BF16),
            pltpu.VMEM((2 + STEPS, 32, TAIL), BF16),
            pltpu.VMEM((3 * PK, 2 * NLIST), BF16),
            pltpu.VMEM((NG6 * LOWL, NLIST), BF16),
            pltpu.VMEM((2, ATOMS, NLIST), F32),
            pltpu.VMEM((ATOMS, LG), F32),
            pltpu.VMEM((2 + STEPS, ATOMS, 3 * LG), F32),
            pltpu.VMEM((STEPS, 2 * KL, NG6 * LOWL), F32),
            pltpu.VMEM((STEPS, 2 * KL, NG6 * LOWL), F32),
            pltpu.VMEM((2, XO, LANES), F32),
            pltpu.VMEM((XO, LANES), F32),
            pltpu.VMEM((2, 8, 256), F32),
            pltpu.VMEM((15, 8, 256), F32),
            pltpu.VMEM((8, 56, 128), F32),
            pltpu.VMEM((7, 56, 128), F32),
            dma((len(sources),)),
            *[dma((5,)) for unused in range(4)],
            *[dma((1,)) for unused in range(2)],
            *[dma((15,)) for unused in range(2)],
            *[dma((7,)) for unused in range(2)],
        ],
        compiler_params=pltpu.CompilerParams(
            collective_id=0, has_side_effects=True, vmem_limit_bytes=60 * 2**20
        ),
    )(*sources)


def solution(mesh):
    return jax.shard_map(
        on_device,
        mesh=mesh,
        in_specs=(P("row", None, None), P("row", None), P(), P(), P(), P()),
        out_specs=(P("row", None, "col"), P("row", "col")),
        check_vma=False,
    )
```

time: 97.3 us -> 49.6 us (0.51)
  the two profiles are of different devices: /device:TPU:56 before, /device:TPU:1 now
where the time goes in v2:
time: 49.6 us; the launch traced here: 49.4 us
  Pallas kernels  46.2 us (93%)
  local copies, waits for them, and re-layouts  2.58 us (5%)
  between operations  0.64 us (1%)
    pallas_call x1, Pallas kernels, on_device(): pl.pallas_call(kernel, out_shape=(jax.ShapeDtypeStruct((1, N, CHUNK), F32...  46.2 us
    pallas_call x1, local copies, waits for them, and re-layouts, on_device(): pl.pallas_call(kernel, out_shape=(jax.ShapeDtypeStruct((1, N, CHUNK), F32...  1.43 us
    unnamed x1, local copies, waits for them, and re-layouts  1.14 us

profile of v2, /device:TPU:1, one launch (start us, length us, event | category | flops | bytes accessed | tf_op | source)
XLA Modules:
  0.0 49.4 jit_solution(4287430776577351688)
XLA Ops:
  0.6 46.2 %shard_map.158 = (f32[1,36,162]{2,1,0:T(8,128)}, f32[1,32]{1,0:T(1,128)}) custom-call(bf16[1,36,1296]{2,1,0:T(8,128)(2,1)} %refs_0_.1, bf16[1,256]{1,0:T(2,128)(2,1)} %refs_1_.1, f32[2,2,64,1024]{3,2,1,0:T(8,128)} %refs_2_.1, s32[1,32]{1,0:T(1,128)} %bitcast.3, f32[3,32]{1,0:T(4,128)} %refs_4_.1, s32[1,1024]{1,0:T(1,128)} %bitcast.2, ...), custom_call_target="tpu_custom_call" | custom-call | tf_op jit(solution)/shard_map/pallas_call | solution.py:529
  46.8 1.4 %copy.17 = f32[1,36,162]{2,0,1:T(1,128)} copy(f32[1,36,162]{2,1,0:T(8,128)} %get-tuple-element.2) | data formatting | bytes 46656 | tf_op jit(solution)/shard_map/pallas_call | solution.py:529
  48.2 1.1 %copy.19 = f32[1,32]{1,0:T(1,128)} copy(f32[1,32]{1,0:T(1,128)} %get-tuple-element.7) | data formatting | bytes 256

commit v3 on v2

--- a/solution.py
+++ b/solution.py
@@ -28,10 +28,30 @@
 F32, BF16 = jnp.float32, jnp.bfloat16
 
 OFFSETS = [
-    *[[(1, j), (-1, (j + 1) % 4), (3, (j + 2) % 4), (-3, (j + 3) % 4)] for j in range(4)],
-    *[[(2, j), (-2, 1 ^ j), (2, 2 ^ j), (-2, 3 ^ j)] for j in range(2)],
-    *[[(0, j), (4, 1 ^ j), (0, 2 ^ j), (4, 3 ^ j)] for j in range(2)],
+    [(1, -1), (3, 0), (-1, 2), (-3, -1)],
+    [(-1, 1), (-3, 0), (1, 2), (3, 1)],
+    [(-2, 0), (2, -1), (2, 2), (-2, -1)],
+    [(2, 0), (-2, 1), (-2, 2), (2, 1)],
+    [(1, 0), (-1, -1), (-3, 2), (3, -1)],
+    [(-1, 0), (1, 1), (3, 2), (-3, 1)],
+    [(0, 0), (0, -1), (4, 2), (4, -1)],
+    [(0, 2), (0, 1), (4, 0), (4, 1)],
 ]
+
+
+def make_targets():
+    targets = []
+    for col in range(8):
+        mine = []
+        for to in (col, col ^ 1):
+            for e, (dz, dy) in enumerate(OFFSETS[to]):
+                if (dy == 0) == (to == col):
+                    mine.append((e // 2, abs(dz) + (0, 1, 3, 1)[dy % 4], to, e % 2, dz, dy))
+        targets.append([(to, n, k, dz, dy) for n, unused, to, k, dz, dy in sorted(mine)])
+    return targets
+
+
+TARGETS = make_targets()
 
 
 def split_np(a):
@@ -95,30 +115,32 @@
                 kern[q * KR + row_of(pair, kx), :216] = np.where(n2 > 0, N**1.5 / 4 / np.maximum(n2, 1), 0)
     packed = [(s, l, m) for s in range(NSPEC) for l in range(NH) for m in range(l, NH)]
     sel = np.zeros((PK, NSPEC * NH * NH), np.float32)
-    rep = np.zeros((256, 768), np.float32)
+    rep = np.zeros((NH, 768), np.float32)
     rsum = np.zeros((256, 256), np.float32)
     weight = np.zeros((NSPEC, LG), np.float32)
     kk = np.arange(256) % NH
+    k8 = np.arange(NH)
+    fold = kk[:, None] == k8[None, :]
     for p, (s, l, m) in enumerate(packed):
         sel[p, s * 64 + l * 8 + m] += 0.5
         sel[p, s * 64 + m * 8 + l] += 0.5
         for b in range(3):
-            rep[kk == l, PK * b + p] = 1
-            rep[kk == m, LG + PK * b + p] = 1
+            rep[k8 == l, PK * b + p] = 1
+            rep[k8 == m, LG + PK * b + p] = 1
             weight[s, PK * b + p] = 0.5 if l == m else 1.0
-        rep[kk == m, 2 * LG + p] = 1
+        rep[k8 == m, 2 * LG + p] = 1
         rsum[p, kk == l] = 1
         if l != m:
-            rep[kk == l, 2 * LG + PK + p] = 1
+            rep[k8 == l, 2 * LG + PK + p] = 1
             rsum[PK + p, kk == m] = 1
     return dict(
-        fwd=fwd, inv=inv, dft=dft, tw=tw, kern=kern, sel=sel.astype(bf), rep=rep.astype(bf), rsum=rsum.astype(bf),
+        fwd=fwd, inv=inv, dft=dft, tw=tw, kern=kern, sel=sel.astype(bf), rep=rep.astype(bf), rsum=rsum.astype(bf), fold=fold.astype(bf),
         weight=np.concatenate([weight, np.zeros((6, LG), np.float32)]),
     )
 
 
 TABLES = make_tables()
-TABLE_NAMES = ("fwd", "inv", "dft", "tw", "kern", "sel", "rep", "rsum", "weight")
+TABLE_NAMES = ("fwd", "inv", "dft", "tw", "kern", "sel", "rep", "rsum", "fold", "weight")
 
 
 def split(a):
@@ -198,13 +220,13 @@
     return rows == kx, rows == kx + 11
 
 
-def augment(glist_ref, qz_ref, exp_ref, choose_ref, phase_ref, yzt_ref, faug_ref):
+def augment(n, glist_ref, qz_ref, exp_ref, choose_ref, phase_ref, yzt_ref, faug_ref):
     lane = lax.broadcasted_iota(jnp.int32, (ATOMS, LG), 1)
     middle = jnp.logical_and(lane >= PK, lane < 2 * PK)
     mixed = []
-    for t in range(STEPS):
+    for t in range(2):
         for i in range(2):
-            a, b = exp_ref[i], exp_ref[2 + t]
+            a, b = exp_ref[i], exp_ref[2 + 2 * n + t]
             full = (a[:, :LG] * b[:, LG : 2 * LG] + b[:, :LG] * a[:, LG : 2 * LG]) * choose_ref[...]
             hi = full.astype(BF16).astype(F32)
             mixed.append(jnp.where(middle, full - hi, hi).astype(BF16)[:, : 3 * PK])
@@ -213,7 +235,7 @@
     z_im = mm(mixed, qz_ref[:, NLIST:])
     first, second = kx_rows(glist_ref)
     spread = []
-    for t in range(STEPS):
+    for t in range(2):
         re, im = [], []
         for i in range(2):
             at = (2 * t + i) * ATOMS
@@ -226,9 +248,9 @@
     both = jnp.concatenate([hi, lo], axis=0)
     for base in range(0, NG6 * LOWL, LG):
         part = mm_nt(both, yzt_ref[base : base + LG, :])
-        part = part[:192] + part[192:]
-        for t in range(STEPS):
-            faug_ref[t, :, base : base + LG] = part[48 * t : 48 * (t + 1)]
+        part = part[:96] + part[96:]
+        for t in range(2):
+            faug_ref[2 * n + t, :, base : base + LG] = part[48 * t : 48 * (t + 1)]
 
 
 def batch(t, band_ref, faug_ref, wst_ref, acc_ref, tabs):
@@ -277,13 +299,13 @@
     acc_ref[1] += pot[XO:] * other[:XO]
 
 
-def slopes(glist_ref, qz_ref, exp_ref, choose_ref, phase_ref, yzt_ref, wst_ref):
-    hi, lo = split(wst_ref[...].reshape(STEPS * 2 * KL, NG6 * LOWL))
+def slopes(n, glist_ref, qz_ref, exp_ref, choose_ref, phase_ref, yzt_ref, wst_ref):
+    hi, lo = split(wst_ref[2 * n : 2 * n + 2].reshape(4 * KL, NG6 * LOWL))
     picked = mm(jnp.concatenate([hi, lo], axis=0), yzt_ref[...])
-    picked = picked[:192] + picked[192:]
+    picked = picked[:96] + picked[96:]
     first, second = kx_rows(glist_ref)
     cross = []
-    for t in range(STEPS):
+    for t in range(2):
         for mask in (first, second):
             at = t * 2 * KL
             wr = jnp.sum(jnp.where(mask, picked[at : at + KL], 0.0), axis=0, keepdims=True)
@@ -293,17 +315,17 @@
             cross.append(jnp.concatenate([re, im], axis=1))
     hi, lo = split(jnp.concatenate(cross, axis=0))
     full = mm_nt(jnp.concatenate([hi, lo], axis=0), qz_ref[...])
-    high, low = full[:256], full[256:]
+    high, low = full[:128], full[128:]
     rest = high[:, 2 * PK :]
     slope = (high[:, : 2 * PK] + low[:, : 2 * PK] + jnp.concatenate([rest, rest], axis=1)) * (2.0 * AUG / N**3)
-    slope = jnp.concatenate([slope, jnp.zeros((256, LG - 2 * PK), F32)], axis=1)
+    slope = jnp.concatenate([slope, jnp.zeros((128, LG - 2 * PK), F32)], axis=1)
     chosen = jnp.where(choose_ref[...] > 0.0, 1.0, 0.0)
     sums = []
     for i in range(2):
         total = jnp.zeros((ATOMS, LG), F32)
-        for t in range(STEPS):
+        for t in range(2):
             at = (2 * t + i) * ATOMS
-            total = total + slope[at : at + ATOMS] * exp_ref[2 + t][:, 2 * LG :]
+            total = total + slope[at : at + ATOMS] * exp_ref[2 + 2 * n + t][:, 2 * LG :]
         sums.append(total * chosen)
     return sums
 
@@ -314,13 +336,20 @@
     return jnp.sum(jnp.where(atom_of_lane(), full, 0.0), axis=0, keepdims=True)
 
 
-def pack_tail(rows):
-    return jnp.concatenate([rows[:, TAIL * j : TAIL * (j + 1)] for j in range(4)], axis=0)
-
-
-def unpack_tail(tail):
-    rows = jnp.concatenate([tail[4 * j : 4 * (j + 1)] for j in range(4)], axis=1)
-    return jnp.concatenate([rows, jnp.zeros((12, LANES), F32)], axis=0)
+def pack_tail(rows, coefs):
+    rows = jnp.concatenate([rows[:, 324 * j : 324 * (j + 1)] for j in range(4)], axis=0)
+    return jnp.concatenate([rows, coefs[:16], coefs[16:], jnp.zeros((16, TAIL - 340), F32)], axis=1)
+
+
+def tail_coefs(tail):
+    return jnp.concatenate([tail[:, 324:332], tail[:, 332:340]], axis=0)
+
+
+def spread_band(main, tail):
+    rows = jnp.concatenate([tail[4 * j : 4 * (j + 1), :324] for j in range(4)], axis=1)
+    full = jnp.concatenate([main, rows, jnp.zeros((12, 1296), F32)], axis=0)
+    zero = jnp.zeros((XB, LG - 216), F32)
+    return jnp.concatenate([p for g in range(NG6) for p in (full[:, 216 * g : 216 * (g + 1)], zero)], axis=1)
 
 
 def columns(total, c):
@@ -350,7 +379,7 @@
     scratch = refs[8 + nt :]
     bands_ref, coef_ref, q_ref, species_ref, positions_ref, glist_ref = scratch[:6]
     tabs = dict(zip(TABLE_NAMES, scratch[6 : 6 + nt]))
-    (band_ref, tail_ref, qz_ref, yzt_ref, phase_ref, choose_ref, exp_ref, faug_ref, wst_ref,
+    (band_ref, raw_ref, tail_ref, qz_ref, yzt_ref, phase_ref, choose_ref, exp_ref, faug_ref, wst_ref,
      acc_ref, got_ref, pgive_ref, pgot_ref, chunk_ref, chunks_ref,
      load_sem, tail_send, tail_recv, band_send, band_recv, sum_send, sum_recv, coef_send, coef_recv,
      chunk_send, chunk_recv) = scratch[6 + nt :]
@@ -360,19 +389,22 @@
     def pick(values):
         return sum(jnp.where(col == c, v, 0) for c, v in enumerate(values))
 
-    def at(dz, dy, k):
-        return (((zed + dz + 16) % 8 * 4 + (wide + dy + 8) % 4) * 2 + k, col)
-
-    sibling = at(0, 0, 1 - core)
+    def at(dz, dy, k, c):
+        return (((zed + dz + 16) % 8 * 4 + (wide + dy + 8) % 4) * 2 + k, c)
+
+    sibling = at(0, 0, 1 - core, col)
     targets, origins = [], []
     for m in range(4):
-        targets.append(at(-pick([o[m][0] for o in OFFSETS]), -pick([o[m][1] for o in OFFSETS]), m % 2))
+        to, n, k, dz, dy = (pick([entries[m][e] for entries in TARGETS]) for e in range(5))
+        targets.append((at(-dz, -dy, k, to), 2 * n + core))
     for n in range(2):
-        dz, dy = (
-            pick([o[2 * n][e] for o in OFFSETS]) * (1 - core) + pick([o[2 * n + 1][e] for o in OFFSETS]) * core
-            for e in range(2)
+        dz, dy, other = (
+            pick([e[2 * n][0] for e in OFFSETS]) * (1 - core) + pick([e[2 * n + 1][0] for e in OFFSETS]) * core,
+            pick([e[2 * n][1] for e in OFFSETS]) * (1 - core) + pick([e[2 * n + 1][1] for e in OFFSETS]) * core,
+            pick([int(e[2 * n][1] != 0) for e in OFFSETS]) * (1 - core)
+            + pick([int(e[2 * n + 1][1] != 0) for e in OFFSETS]) * core,
         )
-        origins += [at(dz, dy, k) for k in range(2)]
+        origins += [at(dz, dy, k, col + other * (1 - 2 * (col % 2))) for k in range(2)]
     home = jnp.logical_and(col == 6, core == 0)
     away = jnp.logical_not(home)
     peers = [(row, (col + step) % 8) for step in range(1, 8)]
@@ -389,6 +421,7 @@
     for partner in others:
         greet(partner)
 
+    names = ("bands", "projections", "qfunc", "species", "positions", "glist", *TABLE_NAMES)
     loads = [
         pltpu.make_async_copy(src, dst, load_sem.at[n]) for n, (src, dst) in enumerate(zip(sources, scratch[: 6 + nt]))
     ]
@@ -403,37 +436,32 @@
 
     loads[0].wait()
     loads[1].wait()
-    field = bands_ref[0].astype(F32)
-    zero = jnp.zeros((N, LG - 216), F32)
-    field = jnp.concatenate(
-        [piece for g in range(NG6) for piece in (field[:, 216 * g : 216 * (g + 1)], zero)], axis=1
-    )
-    band_ref[0, 0:32, :] = field[:32].astype(BF16)
-    tail = pack_tail(field[32:36])
-    coef_rows = jnp.concatenate([coef_ref[...].astype(F32), jnp.zeros((1, TAIL - 256), F32)], axis=1)
-    tail = jnp.concatenate([tail, coef_rows, jnp.zeros((15, TAIL), F32)], axis=0)
-    tail_ref[0] = tail.astype(BF16)
+    loads[names.index("fold")].wait()
+    own = jnp.where(atom_of_lane(), coef_ref[...].astype(F32), 0.0).astype(BF16)
+    tail_ref[0] = pack_tail(bands_ref[0].astype(F32)[32:36], mm(own, tabs["fold"][...])).astype(BF16)
+    main = bands_ref.at[0, pl.ds(0, 32)]
 
     pl.semaphore_wait(barrier, len(others) + 1 - home.astype(jnp.int32))
     tails = [remote(tail_ref.at[0], tail_ref.at[1], sibling, tail_send, tail_recv, 4)]
-    fields = [remote(band_ref.at[0, pl.ds(0, 32)], band_ref.at[1, pl.ds(0, 32)], sibling, band_send, band_recv, 4)]
-    for m in range(4):
-        t = 2 * (m // 2) + core
-        tails.append(remote(tail_ref.at[0], tail_ref.at[2 + t], targets[m], tail_send, tail_recv, m, t))
-        fields.append(
-            remote(
-                band_ref.at[0, pl.ds(0, 32)], band_ref.at[2 + t, pl.ds(0, 32)], targets[m], band_send, band_recv, m, t
-            )
-        )
-    for group in (tails, fields):
-        for n, copy in enumerate(group):
+    fields = [remote(main, raw_ref.at[1], sibling, band_send, band_recv, 4)]
+    for m, (to, t) in enumerate(targets):
+        tails.append(remote(tail_ref.at[0], tail_ref.at[2 + t], to, tail_send, tail_recv, m, t))
+        fields.append(remote(main, raw_ref.at[2 + t], to, band_send, band_recv, m, t))
+
+    def each(group, numbers, act):
+        for n in numbers:
             if n == 1:
-                pl.when(away)(copy.start)
+                pl.when(away)(lambda: act(group[n]))
             else:
-                copy.start()
-
-    for load in loads[2:]:
-        load.wait()
+                act(group[n])
+
+    for numbers in ((0, 1, 2), (3, 4)):
+        for group in (tails, fields):
+            each(group, numbers, lambda copy: copy.start())
+
+    for n, load in enumerate(loads):
+        if n > 1 and names[n] != "fold":
+            load.wait()
     setup_lists(glist_ref, positions_ref, species_ref, tabs["weight"], yzt_ref, phase_ref, choose_ref)
     acc_ref[...] = jnp.zeros_like(acc_ref)
     for c in range(2):
@@ -448,36 +476,44 @@
             device_id_type=mesh_id,
         ).wait_recv()
 
-    def home_tail():
+    def unpack(b):
+        band_ref[b] = spread_band(raw_ref[b].astype(F32), tail_ref[b].astype(F32)).astype(BF16)
+
+    def expand(b):
+        exp_ref[b] = mm(tail_coefs(tail_ref[b].astype(F32)).astype(BF16), tabs["rep"][...])
+
+    def copy_home():
         tail_ref[2] = tail_ref[0]
-
-    pl.when(home)(home_tail)
-    for b in range(2 + STEPS):
-        if b:
-            wait = functools.partial(arrived, tail_ref.at[0], tail_ref.at[b], tail_recv, (b + 3) % 5)
-            if b == 2:
+        raw_ref[2] = bands_ref[0, 0:32, :]
+
+    pl.when(home)(copy_home)
+    raw_ref[0] = bands_ref[0, 0:32, :]
+    unpack(0)
+    expand(0)
+    arrived(tail_ref.at[0], tail_ref.at[1], tail_recv, 4)
+    expand(1)
+    arrived(main, raw_ref.at[1], band_recv, 4)
+    unpack(1)
+
+    def step(t, carry):
+        pl.when(jnp.logical_or(away, t > 0))(lambda: arrived(main, raw_ref.at[2 + t], band_recv, t))
+        unpack(2 + t)
+        batch(t, band_ref, faug_ref, wst_ref, acc_ref, tabs)
+        return carry
+
+    sums = []
+    for n in range(2):
+        for t in (2 * n, 2 * n + 1):
+            wait = functools.partial(arrived, tail_ref.at[0], tail_ref.at[2 + t], tail_recv, t)
+            if t == 0:
                 pl.when(away)(wait)
             else:
                 wait()
-        tail = tail_ref[b].astype(F32)
-        band_ref[b, 32:48, :] = unpack_tail(tail[:16]).astype(BF16)
-        spread = jnp.where(atom_of_lane(), tail[16:17, :256], 0.0).astype(BF16)
-        exp_ref[b] = mm(spread, tabs["rep"][...])
-    augment(glist_ref, qz_ref, exp_ref, choose_ref, phase_ref, yzt_ref, faug_ref)
-
-    def home_band():
-        band_ref[2, 0:32, :] = band_ref[0, 0:32, :]
-
-    pl.when(home)(home_band)
-    arrived(band_ref.at[0, pl.ds(0, 32)], band_ref.at[1, pl.ds(0, 32)], band_recv, 4)
-
-    def step(t, carry):
-        wait = lambda: arrived(band_ref.at[0, pl.ds(0, 32)], band_ref.at[2 + t, pl.ds(0, 32)], band_recv, t)
-        pl.when(jnp.logical_or(away, t > 0))(wait)
-        batch(t, band_ref, faug_ref, wst_ref, acc_ref, tabs)
-        return carry
-
-    lax.fori_loop(0, STEPS, step, 0)
+            expand(2 + t)
+        augment(n, glist_ref, qz_ref, exp_ref, choose_ref, phase_ref, yzt_ref, faug_ref)
+        lax.fori_loop(2 * n, 2 * n + 2, step, 0)
+        if n == 0:
+            sums.append(slopes(n, glist_ref, qz_ref, exp_ref, choose_ref, phase_ref, yzt_ref, wst_ref))
     give = remote(acc_ref.at[1], got_ref, sibling, sum_send, sum_recv, 0)
     give.start()
     give.wait_recv()
@@ -488,8 +524,8 @@
     for n, to in enumerate(peers):
         chunks.append(remote(chunk_ref.at[to[1]], chunks_ref.at[n], to, chunk_send, chunk_recv, n))
         chunks[-1].start()
-    sums = slopes(glist_ref, qz_ref, exp_ref, choose_ref, phase_ref, yzt_ref, wst_ref)
-    rows = [coef_row(packed, tabs["rsum"][...]) for packed in sums]
+    sums.append(slopes(1, glist_ref, qz_ref, exp_ref, choose_ref, phase_ref, yzt_ref, wst_ref))
+    rows = [coef_row(sums[0][i] + sums[1][i], tabs["rsum"][...]) for i in range(2)]
     for i in range(2):
         pgive_ref[i] = jnp.broadcast_to(rows[i], (8, 256))
     coefs = []
@@ -501,21 +537,17 @@
         copy.wait_recv()
         whole = whole + chunks_ref[n]
     whole = whole * -0.5
-    out_ref[0, :, 0:128] = whole[:N]
-    out_ref[0, 0:16, 128:CHUNK] = whole[40:56, 0:34]
-    out_ref[0, 16:32, 128:CHUNK] = whole[40:56, 34:68]
-    out_ref[0, 32:36, 128:CHUNK] = whole[40:44, 68:102]
+    out_ref[:, 0, 0:128] = whole[:N]
+    out_ref[0:16, 0, 128:CHUNK] = whole[40:56, 0:34]
+    out_ref[16:32, 0, 128:CHUNK] = whole[40:56, 34:68]
+    out_ref[32:36, 0, 128:CHUNK] = whole[40:44, 68:102]
     proj = rows[0]
     for n, copy in enumerate(coefs):
         copy.wait_recv()
         proj = proj + pgot_ref[n, 0:1, :]
     proj_ref[...] = -0.5 * sum(jnp.where(col == c, proj[:, 32 * c : 32 * (c + 1)], 0.0) for c in range(8))
     for group in (tails, fields):
-        for n, copy in enumerate(group):
-            if n == 1:
-                pl.when(away)(copy.wait_send)
-            else:
-                copy.wait_send()
+        each(group, range(5), lambda copy: copy.wait_send())
     for copy in [give] + chunks + coefs:
         copy.wait_send()
 
@@ -526,15 +558,16 @@
     sources = [bands, projections, qfunc, species.reshape(1, ATOMS), positions, glist.reshape(1, NLIST)]
     sources += [jnp.asarray(TABLES[name]) for name in TABLE_NAMES]
     dma = pltpu.SemaphoreType.DMA
-    return pl.pallas_call(
+    grid, proj = pl.pallas_call(
         kernel,
-        out_shape=(jax.ShapeDtypeStruct((1, N, CHUNK), F32), jax.ShapeDtypeStruct((1, 32), F32)),
+        out_shape=(jax.ShapeDtypeStruct((N, 1, CHUNK), F32), jax.ShapeDtypeStruct((1, 32), F32)),
         in_specs=[hbm] * len(sources),
         out_specs=(vm, vm),
         scratch_shapes=[
             *[pltpu.VMEM(t.shape, t.dtype) for t in sources],
             pltpu.VMEM((2 + STEPS, XB, LANES), BF16),
-            pltpu.VMEM((2 + STEPS, 32, TAIL), BF16),
+            pltpu.VMEM((2 + STEPS, 32, 1296), BF16),
+            pltpu.VMEM((2 + STEPS, 16, TAIL), BF16),
             pltpu.VMEM((3 * PK, 2 * NLIST), BF16),
             pltpu.VMEM((NG6 * LOWL, NLIST), BF16),
             pltpu.VMEM((2, ATOMS, NLIST), F32),
@@ -558,6 +591,7 @@
             collective_id=0, has_side_effects=True, vmem_limit_bytes=60 * 2**20
         ),
     )(*sources)
+    return (jnp.swapaxes(grid, 0, 1), proj)
 
 
 def solution(mesh):

time: 49.6 us -> 48.8 us (0.984); the launches traced: 49.4 us -> 48 us
  Pallas kernels: 46.2 us -> 44.8 us
    pallas_call x1 -> x0, local copies, waits for them, and re-layouts: 1.43 us -> none  [on_device(): pl.pallas_call(kernel, out_shape=(jax.ShapeDtypeStruct((1, N, CHUNK), F32...]
    unnamed x1 -> x2, local copies, waits for them, and re-layouts: 1.14 us -> 2.53 us
    pallas_call x1, Pallas kernels: 46.2 us -> 44.8 us  [on_device(): pl.pallas_call(kernel, out_shape=(jax.ShapeDtypeStruct((N, 1, CHUNK), F32...]
where the time goes in v3:
time: 48.8 us; the launch traced here: 48 us
  Pallas kernels  44.8 us (92%)
  local copies, waits for them, and re-layouts  2.53 us (5%)
  between operations  0.64 us (1%)
    pallas_call x1, Pallas kernels, on_device(): pl.pallas_call(kernel, out_shape=(jax.ShapeDtypeStruct((N, 1, CHUNK), F32...  44.8 us
    unnamed x2, local copies, waits for them, and re-layouts  2.53 us

profile of v3, /device:TPU:1, one launch (start us, length us, event | category | flops | bytes accessed | tf_op | source)
XLA Modules:
  0.0 48.0 jit_solution(16793129231493861270)
XLA Ops:
  0.6 44.8 %shard_map.167 = (f32[36,1,162]{2,1,0:T(1,128)}, f32[1,32]{1,0:T(1,128)}) custom-call(bf16[1,36,1296]{2,1,0:T(8,128)(2,1)} %refs_0_.1, bf16[1,256]{1,0:T(2,128)(2,1)} %refs_1_.1, f32[2,2,64,1024]{3,2,1,0:T(8,128)} %refs_2_.1, s32[1,32]{1,0:T(1,128)} %bitcast.5, f32[3,32]{1,0:T(4,128)} %refs_4_.1, s32[1,1024]{1,0:T(1,128)} %bitcast.4, ...), custom_call_target="tpu_custom_call" | custom-call | tf_op jit(solution)/shard_map/pallas_call | solution.py:561
  45.5 1.4 %copy.20 = f32[1,36,162]{2,0,1:T(1,128)} copy(f32[1,36,162]{2,0,1:T(1,128)} %bitcast.3) | data formatting | bytes 46656
  46.8 1.1 %copy.21 = f32[1,32]{1,0:T(1,128)} copy(f32[1,32]{1,0:T(1,128)} %get-tuple-element.9) | data formatting | bytes 256

commit v4 on v3

--- a/solution.py
+++ b/solution.py
@@ -408,7 +408,6 @@
     home = jnp.logical_and(col == 6, core == 0)
     away = jnp.logical_not(home)
     peers = [(row, (col + step) % 8) for step in range(1, 8)]
-    cousins = [(sibling[0], (col + step) % 8) for step in range(1, 8)]
     mesh_id = pl.DeviceIdType.MESH
 
     barrier = pltpu.get_barrier_semaphore()
@@ -417,7 +416,7 @@
         pl.semaphore_signal(barrier, inc=1, device_id=partner, device_id_type=mesh_id)
 
     pl.when(away)(lambda: greet(origins[0]))
-    others = origins[1:] + [sibling] + peers + cousins
+    others = origins[1:] + [sibling] + peers
     for partner in others:
         greet(partner)
 
@@ -516,22 +515,23 @@
             sums.append(slopes(n, glist_ref, qz_ref, exp_ref, choose_ref, phase_ref, yzt_ref, wst_ref))
     give = remote(acc_ref.at[1], got_ref, sibling, sum_send, sum_recv, 0)
     give.start()
+    sums.append(slopes(1, glist_ref, qz_ref, exp_ref, choose_ref, phase_ref, yzt_ref, wst_ref))
+    rows = [coef_row(sums[0][i] + sums[1][i], tabs["rsum"][...]) for i in range(2)]
+    pgive_ref[...] = jnp.broadcast_to(rows[1], (8, 256))
+    coefs = remote(pgive_ref, pgot_ref, sibling, coef_send, coef_recv, 0)
+    coefs.start()
     give.wait_recv()
     total = acc_ref[0] + got_ref[...]
     for c in range(8):
         chunk_ref[c] = pack_chunk(total, c)
+    coefs.wait_recv()
+    proj = rows[0] + pgot_ref[0:1, :]
+    for c in range(8):
+        chunk_ref[c, N : N + 1, 0:32] = proj[:, 32 * c : 32 * (c + 1)]
     chunks = []
     for n, to in enumerate(peers):
         chunks.append(remote(chunk_ref.at[to[1]], chunks_ref.at[n], to, chunk_send, chunk_recv, n))
         chunks[-1].start()
-    sums.append(slopes(1, glist_ref, qz_ref, exp_ref, choose_ref, phase_ref, yzt_ref, wst_ref))
-    rows = [coef_row(sums[0][i] + sums[1][i], tabs["rsum"][...]) for i in range(2)]
-    for i in range(2):
-        pgive_ref[i] = jnp.broadcast_to(rows[i], (8, 256))
-    coefs = []
-    for n, to in enumerate(peers + [sibling] + cousins):
-        coefs.append(remote(pgive_ref.at[0 if n < 7 else 1], pgot_ref.at[n], to, coef_send, coef_recv, n))
-        coefs[-1].start()
     whole = chunk_ref[col]
     for n, copy in enumerate(chunks):
         copy.wait_recv()
@@ -541,15 +541,22 @@
     out_ref[0:16, 0, 128:CHUNK] = whole[40:56, 0:34]
     out_ref[16:32, 0, 128:CHUNK] = whole[40:56, 34:68]
     out_ref[32:36, 0, 128:CHUNK] = whole[40:44, 68:102]
-    proj = rows[0]
-    for n, copy in enumerate(coefs):
-        copy.wait_recv()
-        proj = proj + pgot_ref[n, 0:1, :]
-    proj_ref[...] = -0.5 * sum(jnp.where(col == c, proj[:, 32 * c : 32 * (c + 1)], 0.0) for c in range(8))
+    proj_ref[...] = whole[N : N + 1, 0:32]
     for group in (tails, fields):
         each(group, range(5), lambda copy: copy.wait_send())
-    for copy in [give] + chunks + coefs:
+    for copy in [give, coefs] + chunks:
         copy.wait_send()
+
+
+def hand_over(grid_ref, proj_ref, grid_out, proj_out, sem):
+    copies = [
+        pltpu.make_async_copy(src, dst, sem.at[n])
+        for n, (src, dst) in enumerate(((grid_ref, grid_out), (proj_ref, proj_out)))
+    ]
+    for copy in copies:
+        copy.start()
+    for copy in copies:
+        copy.wait()
 
 
 def on_device(bands, projections, qfunc, species, positions, glist):
@@ -577,20 +584,27 @@
             pltpu.VMEM((STEPS, 2 * KL, NG6 * LOWL), F32),
             pltpu.VMEM((2, XO, LANES), F32),
             pltpu.VMEM((XO, LANES), F32),
-            pltpu.VMEM((2, 8, 256), F32),
-            pltpu.VMEM((15, 8, 256), F32),
+            pltpu.VMEM((8, 256), F32),
+            pltpu.VMEM((8, 256), F32),
             pltpu.VMEM((8, 56, 128), F32),
             pltpu.VMEM((7, 56, 128), F32),
             dma((len(sources),)),
             *[dma((5,)) for unused in range(4)],
-            *[dma((1,)) for unused in range(2)],
-            *[dma((15,)) for unused in range(2)],
+            *[dma((1,)) for unused in range(4)],
             *[dma((7,)) for unused in range(2)],
         ],
         compiler_params=pltpu.CompilerParams(
             collective_id=0, has_side_effects=True, vmem_limit_bytes=60 * 2**20
         ),
     )(*sources)
+    grid, proj = pl.pallas_call(
+        hand_over,
+        out_shape=(jax.ShapeDtypeStruct((N, 1, CHUNK), F32), jax.ShapeDtypeStruct((1, 32), F32)),
+        in_specs=[hbm] * 2,
+        out_specs=(hbm, hbm),
+        scratch_shapes=[dma((2,))],
+        compiler_params=pltpu.CompilerParams(vmem_limit_bytes=60 * 2**20),
+    )(grid, proj)
     return (jnp.swapaxes(grid, 0, 1), proj)
 
 

time: 48.8 us -> 48 us (0.984); the launches traced: 48 us -> 47.9 us
  local copies, waits for them, and re-layouts: 2.53 us -> 0 us
  Pallas kernels: 44.8 us -> 47.2 us
    unnamed x2 -> x0, local copies, waits for them, and re-layouts: 2.53 us -> none
    pallas_call x0 -> x1, Pallas kernels: none -> 2.25 us  [on_device(): pl.pallas_call(hand_over, out_shape=(jax.ShapeDtypeStruct((N, 1, CHUNK),...]
where the time goes in v4:
time: 48 us; the launch traced here: 47.9 us
  Pallas kernels  47.2 us (98%)
  between operations  0.64 us (1%)
    pallas_call x1, Pallas kernels, on_device(): pl.pallas_call(kernel, out_shape=(jax.ShapeDtypeStruct((N, 1, CHUNK), F32...  45 us
    pallas_call x1, Pallas kernels, on_device(): pl.pallas_call(hand_over, out_shape=(jax.ShapeDtypeStruct((N, 1, CHUNK),...  2.25 us

profile of v4, /device:TPU:1, one launch (start us, length us, event | category | flops | bytes accessed | tf_op | source)
XLA Modules:
  0.0 47.9 jit_solution(9650748527401525061)
XLA Ops:
  0.6 45.0 %shard_map.167 = (f32[36,1,162]{2,1,0:T(1,128)}, f32[1,32]{1,0:T(1,128)}) custom-call(bf16[1,36,1296]{2,1,0:T(8,128)(2,1)} %refs_0_.1, bf16[1,256]{1,0:T(2,128)(2,1)} %refs_1_.1, f32[2,2,64,1024]{3,2,1,0:T(8,128)} %refs_2_.1, s32[1,32]{1,0:T(1,128)} %bitcast.4, f32[3,32]{1,0:T(4,128)} %refs_4_.1, s32[1,1024]{1,0:T(1,128)} %bitcast.3, ...), custom_call_target="tpu_custom_call" | custom-call | tf_op jit(solution)/shard_map/pallas_call | solution.py:568
  45.6 2.3 %shard_map.168 = (f32[36,1,162]{2,1,0:T(1,128)}, f32[1,32]{1,0:T(1,128)}) custom-call(f32[36,1,162]{2,1,0:T(1,128)} %get-tuple-element.6.grid_ref, f32[1,32]{1,0:T(1,128)} %get-tuple-element.7.proj_ref), custom_call_target="tpu_custom_call" | custom-call | tf_op jit(solution)/shard_map/pallas_call | solution.py:600

commit v5 on v4

--- a/solution.py
+++ b/solution.py
@@ -454,9 +454,9 @@
             else:
                 act(group[n])
 
-    for numbers in ((0, 1, 2), (3, 4)):
-        for group in (tails, fields):
-            each(group, numbers, lambda copy: copy.start())
+    each(tails, range(5), lambda copy: copy.start())
+    each(fields, (0, 1, 2), lambda copy: copy.start())
+    pl.when(core == 0)(lambda: each(fields, (3, 4), lambda copy: copy.start()))
 
     for n, load in enumerate(loads):
         if n > 1 and names[n] != "fold":
@@ -510,7 +510,13 @@
                 wait()
             expand(2 + t)
         augment(n, glist_ref, qz_ref, exp_ref, choose_ref, phase_ref, yzt_ref, faug_ref)
-        lax.fori_loop(2 * n, 2 * n + 2, step, 0)
+        if n == 0:
+            each(fields, (0, 1, 2), lambda copy: copy.wait_send())
+            step(0, 0)
+            pl.when(core == 1)(lambda: each(fields, (3, 4), lambda copy: copy.start()))
+            lax.fori_loop(1, 2, step, 0)
+        else:
+            lax.fori_loop(2, 4, step, 0)
         if n == 0:
             sums.append(slopes(n, glist_ref, qz_ref, exp_ref, choose_ref, phase_ref, yzt_ref, wst_ref))
     give = remote(acc_ref.at[1], got_ref, sibling, sum_send, sum_recv, 0)
@@ -542,8 +548,8 @@
     out_ref[16:32, 0, 128:CHUNK] = whole[40:56, 34:68]
     out_ref[32:36, 0, 128:CHUNK] = whole[40:44, 68:102]
     proj_ref[...] = whole[N : N + 1, 0:32]
-    for group in (tails, fields):
-        each(group, range(5), lambda copy: copy.wait_send())
+    each(tails, range(5), lambda copy: copy.wait_send())
+    each(fields, (3, 4), lambda copy: copy.wait_send())
     for copy in [give, coefs] + chunks:
         copy.wait_send()
 

time: 48 us -> 46.6 us (0.971)
  Pallas kernels: 47.2 us -> 45.8 us
    pallas_call x1, Pallas kernels: 45 us -> 43.6 us  [on_device(): pl.pallas_call(kernel, out_shape=(jax.ShapeDtypeStruct((N, 1, CHUNK), F32...]
where the time goes in v5:
time: 46.6 us; the launch traced here: 46.5 us
  Pallas kernels  45.8 us (98%)
  between operations  0.64 us (1%)
    pallas_call x1, Pallas kernels, on_device(): pl.pallas_call(kernel, out_shape=(jax.ShapeDtypeStruct((N, 1, CHUNK), F32...  43.6 us
    pallas_call x1, Pallas kernels, on_device(): pl.pallas_call(hand_over, out_shape=(jax.ShapeDtypeStruct((N, 1, CHUNK),...  2.25 us

profile of v5, /device:TPU:1, one launch (start us, length us, event | category | flops | bytes accessed | tf_op | source)
XLA Modules:
  0.0 46.5 jit_solution(8129625753094591261)
XLA Ops:
  0.6 43.6 %shard_map.167 = (f32[36,1,162]{2,1,0:T(1,128)}, f32[1,32]{1,0:T(1,128)}) custom-call(bf16[1,36,1296]{2,1,0:T(8,128)(2,1)} %refs_0_.1, bf16[1,256]{1,0:T(2,128)(2,1)} %refs_1_.1, f32[2,2,64,1024]{3,2,1,0:T(8,128)} %refs_2_.1, s32[1,32]{1,0:T(1,128)} %bitcast.4, f32[3,32]{1,0:T(4,128)} %refs_4_.1, s32[1,1024]{1,0:T(1,128)} %bitcast.3, ...), custom_call_target="tpu_custom_call" | custom-call | tf_op jit(solution)/shard_map/pallas_call | solution.py:574
  44.2 2.3 %shard_map.168 = (f32[36,1,162]{2,1,0:T(1,128)}, f32[1,32]{1,0:T(1,128)}) custom-call(f32[36,1,162]{2,1,0:T(1,128)} %get-tuple-element.6.grid_ref, f32[1,32]{1,0:T(1,128)} %get-tuple-element.7.proj_ref), custom_call_target="tpu_custom_call" | custom-call | tf_op jit(solution)/shard_map/pallas_call | solution.py:606

commit v6 on v4

--- a/solution.py
+++ b/solution.py
@@ -27,31 +27,14 @@
 CHUNK = 162
 F32, BF16 = jnp.float32, jnp.bfloat16
 
-OFFSETS = [
-    [(1, -1), (3, 0), (-1, 2), (-3, -1)],
-    [(-1, 1), (-3, 0), (1, 2), (3, 1)],
-    [(-2, 0), (2, -1), (2, 2), (-2, -1)],
-    [(2, 0), (-2, 1), (-2, 2), (2, 1)],
-    [(1, 0), (-1, -1), (-3, 2), (3, -1)],
-    [(-1, 0), (1, 1), (3, 2), (-3, 1)],
-    [(0, 0), (0, -1), (4, 2), (4, -1)],
-    [(0, 2), (0, 1), (4, 0), (4, 1)],
+ITEMS = [
+    [(0, 0, -1, 0), (0, 1, 3, 1), (1, 0, 1, 1), (1, 1, -3, 0)],
+    [(0, 0, -1, 1), (0, 1, 3, 0), (1, 0, 1, 0), (1, 1, -3, 1)],
+    [(0, 0, 2, 0), (0, 1, -2, 1), (1, 0, -2, 0), (1, 1, 2, 1)],
+    [(0, 0, 0, 1), (0, 1, 4, 0), (1, 0, 0, 0), (1, 1, 4, 1)],
 ]
-
-
-def make_targets():
-    targets = []
-    for col in range(8):
-        mine = []
-        for to in (col, col ^ 1):
-            for e, (dz, dy) in enumerate(OFFSETS[to]):
-                if (dy == 0) == (to == col):
-                    mine.append((e // 2, abs(dz) + (0, 1, 3, 1)[dy % 4], to, e % 2, dz, dy))
-        targets.append([(to, n, k, dz, dy) for n, unused, to, k, dz, dy in sorted(mine)])
-    return targets
-
-
-TARGETS = make_targets()
+GIVEN = [[[i for i in items if i[3] == k] for k in range(2)] for items in ITEMS]
+TAKEN = [[[i for i in items if i[0] == k] for k in range(2)] for items in ITEMS]
 
 
 def split_np(a):
@@ -386,27 +369,23 @@
     row, col = lax.axis_index("row"), lax.axis_index("col")
     zed, wide, core = row // 8, row // 2 % 4, row % 2
 
-    def pick(values):
-        return sum(jnp.where(col == c, v, 0) for c, v in enumerate(values))
-
-    def at(dz, dy, k, c):
-        return (((zed + dz + 16) % 8 * 4 + (wide + dy + 8) % 4) * 2 + k, c)
-
-    sibling = at(0, 0, 1 - core, col)
+    far_side = col % 2
+
+    def pick(table, m, e):
+        return sum(
+            jnp.where(jnp.logical_and(col // 2 == c, core == k), table[c][k][m][e], 0) for c in range(4) for k in range(2)
+        )
+
+    def at(dz, dy, k):
+        return (((zed + dz + 16) % 8 * 4 + (wide + dy + 8) % 4) * 2 + k, col)
+
+    sibling = at(0, 0, 1 - core)
+    partner = (at(0, 2 * far_side - 1, core)[0], col + 1 - 2 * far_side)
     targets, origins = [], []
-    for m in range(4):
-        to, n, k, dz, dy = (pick([entries[m][e] for entries in TARGETS]) for e in range(5))
-        targets.append((at(-dz, -dy, k, to), 2 * n + core))
-    for n in range(2):
-        dz, dy, other = (
-            pick([e[2 * n][0] for e in OFFSETS]) * (1 - core) + pick([e[2 * n + 1][0] for e in OFFSETS]) * core,
-            pick([e[2 * n][1] for e in OFFSETS]) * (1 - core) + pick([e[2 * n + 1][1] for e in OFFSETS]) * core,
-            pick([int(e[2 * n][1] != 0) for e in OFFSETS]) * (1 - core)
-            + pick([int(e[2 * n + 1][1] != 0) for e in OFFSETS]) * core,
-        )
-        origins += [at(dz, dy, k, col + other * (1 - 2 * (col % 2))) for k in range(2)]
-    home = jnp.logical_and(col == 6, core == 0)
-    away = jnp.logical_not(home)
+    for m in range(2):
+        k = pick(GIVEN, m, 0)
+        targets.append((at(-pick(GIVEN, m, 2), k + far_side - 1, k), pick(GIVEN, m, 1)))
+        origins.append(at(pick(TAKEN, m, 2), 1 - core - far_side, pick(TAKEN, m, 3)))
     peers = [(row, (col + step) % 8) for step in range(1, 8)]
     mesh_id = pl.DeviceIdType.MESH
 
@@ -415,10 +394,9 @@
     def greet(partner):
         pl.semaphore_signal(barrier, inc=1, device_id=partner, device_id_type=mesh_id)
 
-    pl.when(away)(lambda: greet(origins[0]))
-    others = origins[1:] + [sibling] + peers
-    for partner in others:
-        greet(partner)
+    others = origins + [sibling, partner] + peers
+    for other in others:
+        greet(other)
 
     names = ("bands", "projections", "qfunc", "species", "positions", "glist", *TABLE_NAMES)
     loads = [
@@ -440,23 +418,14 @@
     tail_ref[0] = pack_tail(bands_ref[0].astype(F32)[32:36], mm(own, tabs["fold"][...])).astype(BF16)
     main = bands_ref.at[0, pl.ds(0, 32)]
 
-    pl.semaphore_wait(barrier, len(others) + 1 - home.astype(jnp.int32))
+    pl.semaphore_wait(barrier, len(others))
     tails = [remote(tail_ref.at[0], tail_ref.at[1], sibling, tail_send, tail_recv, 4)]
     fields = [remote(main, raw_ref.at[1], sibling, band_send, band_recv, 4)]
     for m, (to, t) in enumerate(targets):
         tails.append(remote(tail_ref.at[0], tail_ref.at[2 + t], to, tail_send, tail_recv, m, t))
         fields.append(remote(main, raw_ref.at[2 + t], to, band_send, band_recv, m, t))
-
-    def each(group, numbers, act):
-        for n in numbers:
-            if n == 1:
-                pl.when(away)(lambda: act(group[n]))
-            else:
-                act(group[n])
-
-    for numbers in ((0, 1, 2), (3, 4)):
-        for group in (tails, fields):
-            each(group, numbers, lambda copy: copy.start())
+    for copy in tails + fields:
+        copy.start()
 
     for n, load in enumerate(loads):
         if n > 1 and names[n] != "fold":
@@ -481,11 +450,6 @@
     def expand(b):
         exp_ref[b] = mm(tail_coefs(tail_ref[b].astype(F32)).astype(BF16), tabs["rep"][...])
 
-    def copy_home():
-        tail_ref[2] = tail_ref[0]
-        raw_ref[2] = bands_ref[0, 0:32, :]
-
-    pl.when(home)(copy_home)
     raw_ref[0] = bands_ref[0, 0:32, :]
     unpack(0)
     expand(0)
@@ -494,8 +458,15 @@
     arrived(main, raw_ref.at[1], band_recv, 4)
     unpack(1)
 
+    def relay(t, ref, sends, recvs):
+        copy = remote(ref.at[2 + t], ref.at[4 + t], partner, sends, recvs, 2 + t)
+        copy.start()
+        return copy
+
     def step(t, carry):
-        pl.when(jnp.logical_or(away, t > 0))(lambda: arrived(main, raw_ref.at[2 + t], band_recv, t))
+        arrived(main, raw_ref.at[2 + t], band_recv, t)
+        if isinstance(t, int):
+            fields.append(relay(t, raw_ref, band_send, band_recv))
         unpack(2 + t)
         batch(t, band_ref, faug_ref, wst_ref, acc_ref, tabs)
         return carry
@@ -503,16 +474,17 @@
     sums = []
     for n in range(2):
         for t in (2 * n, 2 * n + 1):
-            wait = functools.partial(arrived, tail_ref.at[0], tail_ref.at[2 + t], tail_recv, t)
-            if t == 0:
-                pl.when(away)(wait)
-            else:
-                wait()
+            arrived(tail_ref.at[0], tail_ref.at[2 + t], tail_recv, t)
+            if n == 0:
+                tails.append(relay(t, tail_ref, tail_send, tail_recv))
             expand(2 + t)
         augment(n, glist_ref, qz_ref, exp_ref, choose_ref, phase_ref, yzt_ref, faug_ref)
-        lax.fori_loop(2 * n, 2 * n + 2, step, 0)
         if n == 0:
+            step(0, 0)
+            step(1, 0)
             sums.append(slopes(n, glist_ref, qz_ref, exp_ref, choose_ref, phase_ref, yzt_ref, wst_ref))
+        else:
+            lax.fori_loop(2, 4, step, 0)
     give = remote(acc_ref.at[1], got_ref, sibling, sum_send, sum_recv, 0)
     give.start()
     sums.append(slopes(1, glist_ref, qz_ref, exp_ref, choose_ref, phase_ref, yzt_ref, wst_ref))
@@ -542,9 +514,7 @@
     out_ref[16:32, 0, 128:CHUNK] = whole[40:56, 34:68]
     out_ref[32:36, 0, 128:CHUNK] = whole[40:44, 68:102]
     proj_ref[...] = whole[N : N + 1, 0:32]
-    for group in (tails, fields):
-        each(group, range(5), lambda copy: copy.wait_send())
-    for copy in [give, coefs] + chunks:
+    for copy in tails + fields + [give, coefs] + chunks:
         copy.wait_send()
 
 

time: 48 us -> 41.2 us (0.86)
  Pallas kernels: 47.2 us -> 40.4 us
    pallas_call x1, Pallas kernels: 45 us -> 38.2 us  [on_device(): pl.pallas_call(kernel, out_shape=(jax.ShapeDtypeStruct((N, 1, CHUNK), F32...]
where the time goes in v6:
time: 41.2 us; the launch traced here: 41.1 us
  Pallas kernels  40.4 us (98%)
  between operations  0.64 us (2%)
    pallas_call x1, Pallas kernels, on_device(): pl.pallas_call(kernel, out_shape=(jax.ShapeDtypeStruct((N, 1, CHUNK), F32...  38.2 us
    pallas_call x1, Pallas kernels, on_device(): pl.pallas_call(hand_over, out_shape=(jax.ShapeDtypeStruct((N, 1, CHUNK),...  2.25 us

profile of v6, /device:TPU:1, one launch (start us, length us, event | category | flops | bytes accessed | tf_op | source)
XLA Modules:
  0.0 41.1 jit_solution(15394474876982572870)
XLA Ops:
  0.6 38.2 %shard_map.167 = (f32[36,1,162]{2,1,0:T(1,128)}, f32[1,32]{1,0:T(1,128)}) custom-call(bf16[1,36,1296]{2,1,0:T(8,128)(2,1)} %refs_0_.1, bf16[1,256]{1,0:T(2,128)(2,1)} %refs_1_.1, f32[2,2,64,1024]{3,2,1,0:T(8,128)} %refs_2_.1, s32[1,32]{1,0:T(1,128)} %bitcast.4, f32[3,32]{1,0:T(4,128)} %refs_4_.1, s32[1,1024]{1,0:T(1,128)} %bitcast.3, ...), custom_call_target="tpu_custom_call" | custom-call | tf_op jit(solution)/shard_map/pallas_call | solution.py:538
  38.8 2.3 %shard_map.168 = (f32[36,1,162]{2,1,0:T(1,128)}, f32[1,32]{1,0:T(1,128)}) custom-call(f32[36,1,162]{2,1,0:T(1,128)} %get-tuple-element.6.grid_ref, f32[1,32]{1,0:T(1,128)} %get-tuple-element.7.proj_ref), custom_call_target="tpu_custom_call" | custom-call | tf_op jit(solution)/shard_map/pallas_call | solution.py:570

commit v7 on v6

--- a/solution.py
+++ b/solution.py
@@ -518,15 +518,9 @@
         copy.wait_send()
 
 
-def hand_over(grid_ref, proj_ref, grid_out, proj_out, sem):
-    copies = [
-        pltpu.make_async_copy(src, dst, sem.at[n])
-        for n, (src, dst) in enumerate(((grid_ref, grid_out), (proj_ref, proj_out)))
-    ]
-    for copy in copies:
-        copy.start()
-    for copy in copies:
-        copy.wait()
+def hand_over(grid_ref, proj_ref, grid_out, proj_out):
+    grid_out[...] = grid_ref[...]
+    proj_out[...] = proj_ref[...]
 
 
 def on_device(bands, projections, qfunc, species, positions, glist):
@@ -570,9 +564,8 @@
     grid, proj = pl.pallas_call(
         hand_over,
         out_shape=(jax.ShapeDtypeStruct((N, 1, CHUNK), F32), jax.ShapeDtypeStruct((1, 32), F32)),
-        in_specs=[hbm] * 2,
-        out_specs=(hbm, hbm),
-        scratch_shapes=[dma((2,))],
+        in_specs=[vm] * 2,
+        out_specs=(vm, vm),
         compiler_params=pltpu.CompilerParams(vmem_limit_bytes=60 * 2**20),
     )(grid, proj)
     return (jnp.swapaxes(grid, 0, 1), proj)

time: 41.2 us -> 40.4 us (0.981)
  Pallas kernels: 40.4 us -> 39.6 us
    pallas_call x1, Pallas kernels: 2.25 us -> 1.4 us  [on_device(): pl.pallas_call(hand_over, out_shape=(jax.ShapeDtypeStruct((N, 1, CHUNK),...]
where the time goes in v7:
time: 40.4 us; the launch traced here: 40.2 us
  Pallas kernels  39.6 us (98%)
  between operations  0.64 us (2%)
    pallas_call x1, Pallas kernels, on_device(): pl.pallas_call(kernel, out_shape=(jax.ShapeDtypeStruct((N, 1, CHUNK), F32...  38.2 us
    pallas_call x1, Pallas kernels, on_device(): pl.pallas_call(hand_over, out_shape=(jax.ShapeDtypeStruct((N, 1, CHUNK),...  1.4 us

profile of v7, /device:TPU:1, one launch (start us, length us, event | category | flops | bytes accessed | tf_op | source)
XLA Modules:
  0.0 40.2 jit_solution(7462325202334570056)
XLA Ops:
  0.6 38.2 %shard_map.167 = (f32[36,1,162]{2,1,0:T(1,128)}, f32[1,32]{1,0:T(1,128)}) custom-call(bf16[1,36,1296]{2,1,0:T(8,128)(2,1)} %refs_0_.1, bf16[1,256]{1,0:T(2,128)(2,1)} %refs_1_.1, f32[2,2,64,1024]{3,2,1,0:T(8,128)} %refs_2_.1, s32[1,32]{1,0:T(1,128)} %bitcast.4, f32[3,32]{1,0:T(4,128)} %refs_4_.1, s32[1,1024]{1,0:T(1,128)} %bitcast.3, ...), custom_call_target="tpu_custom_call" | custom-call | tf_op jit(solution)/shard_map/pallas_call | solution.py:532
  38.8 1.4 %shard_map.168 = (f32[36,1,162]{2,1,0:T(1,128)}, f32[1,32]{1,0:T(1,128)}) custom-call(f32[36,1,162]{2,1,0:T(1,128)} %get-tuple-element.6.grid_ref, f32[1,32]{1,0:T(1,128)} %get-tuple-element.7.proj_ref), custom_call_target="tpu_custom_call" | custom-call | tf_op jit(solution)/shard_map/pallas_call | solution.py:564

commit v8 on v7

--- a/solution.py
+++ b/solution.py
@@ -427,8 +427,9 @@
     for copy in tails + fields:
         copy.start()
 
+    late = ("fwd", "inv", "dft", "tw", "kern", "rsum")
     for n, load in enumerate(loads):
-        if n > 1 and names[n] != "fold":
+        if n > 1 and names[n] != "fold" and names[n] not in late:
             load.wait()
     setup_lists(glist_ref, positions_ref, species_ref, tabs["weight"], yzt_ref, phase_ref, choose_ref)
     acc_ref[...] = jnp.zeros_like(acc_ref)
@@ -471,6 +472,8 @@
         batch(t, band_ref, faug_ref, wst_ref, acc_ref, tabs)
         return carry
 
+    for name in late:
+        loads[names.index(name)].wait()
     sums = []
     for n in range(2):
         for t in (2 * n, 2 * n + 1):

time: 40.4 us -> 40.4 us (level)
  no operation moved by 1% of the time
where the time goes in v8:
time: 40.4 us; the launch traced here: 40.2 us
  Pallas kernels  39.6 us (98%)
  between operations  0.64 us (2%)
    pallas_call x1, Pallas kernels, on_device(): pl.pallas_call(kernel, out_shape=(jax.ShapeDtypeStruct((N, 1, CHUNK), F32...  38.2 us
    pallas_call x1, Pallas kernels, on_device(): pl.pallas_call(hand_over, out_shape=(jax.ShapeDtypeStruct((N, 1, CHUNK),...  1.4 us

profile of v8, /device:TPU:1, one launch (start us, length us, event | category | flops | bytes accessed | tf_op | source)
XLA Modules:
  0.0 40.2 jit_solution(16992271831963544741)
XLA Ops:
  0.6 38.2 %shard_map.167 = (f32[36,1,162]{2,1,0:T(1,128)}, f32[1,32]{1,0:T(1,128)}) custom-call(bf16[1,36,1296]{2,1,0:T(8,128)(2,1)} %refs_0_.1, bf16[1,256]{1,0:T(2,128)(2,1)} %refs_1_.1, f32[2,2,64,1024]{3,2,1,0:T(8,128)} %refs_2_.1, s32[1,32]{1,0:T(1,128)} %bitcast.4, f32[3,32]{1,0:T(4,128)} %refs_4_.1, s32[1,1024]{1,0:T(1,128)} %bitcast.3, ...), custom_call_target="tpu_custom_call" | custom-call | tf_op jit(solution)/shard_map/pallas_call | solution.py:535
  38.8 1.4 %shard_map.168 = (f32[36,1,162]{2,1,0:T(1,128)}, f32[1,32]{1,0:T(1,128)}) custom-call(f32[36,1,162]{2,1,0:T(1,128)} %get-tuple-element.6.grid_ref, f32[1,32]{1,0:T(1,128)} %get-tuple-element.7.proj_ref), custom_call_target="tpu_custom_call" | custom-call | tf_op jit(solution)/shard_map/pallas_call | solution.py:567
